TPU v7x, 256 devices: a whole 4x4x8 slice. The times are simulated.
256 devices in a mesh: stream: 16 (over z, core), vert: 4 (over x), span: 4 (over y).
Axes of the slice: x: 4, y: 4, z: 8, core: 2. Of those that a mesh axis runs over, the one named last changes fastest.
Arguments:
- adjoint_source: float32 [3, 128, 48, 1024], P(None, 'stream', 'span', 'vert'), may hold values from -48 to 48
- velocity: float32 [3, 128, 48, 1024], P(None, 'stream', 'span', 'vert'), may hold values from -4 to 4
- penalty: float32 [128, 48, 1024], P('stream', 'span', 'vert'), may hold values from 0.05 to 2
- adjoint_start: float32 [3, 128, 48, 1024], P(None, 'stream', 'span', 'vert'), may hold values from -1800 to 1800
- cell_band: int32 [128, 48, 1024], P('stream', 'span', 'vert'), may hold values from 0 to 255
- tri_band: int32 [32768], P(('stream', 'vert', 'span')), may hold values from 0 to 255
- tri_weight: float32 [32768], P(('stream', 'vert', 'span')), may hold values from 0.5 to 2
Outputs:
- adjoint: float32 [3, 128, 48, 1024], P(None, 'stream', 'span', 'vert')
- tri_grad: float32 [32768], P(('stream', 'vert', 'span'))
All inputs are finite; a program needn't handle non-finite values.
Results may differ from a plain program's by a relative error of at most 0.0003.
Values sent between devices are 32-bit elements; how exact they have to be, the bound alone decides.
A program may use at most 64 MiB of HBM per device.

v0:
```python
import jax
import jax.numpy as jnp
from jax import lax
from jax.sharding import PartitionSpec as P

SWEEPS = 2
NBANDS = 256


stream_coef = 1000.0
stream_conv = 200.0
cross_coef = 0.25
cross_conv = 0.25
shift_coef = 0.5


def padded_2(block, sides, width):
    for axis, dim in sides:
        count = lax.axis_size(axis)
        forward = [(i, i + 1) for i in range(count - 1)]
        backward = [(target, source) for source, target in forward]
        low = lax.ppermute(
            lax.slice_in_dim(block, block.shape[dim] - width, None, axis=dim), axis, forward
        )
        high = lax.ppermute(lax.slice_in_dim(block, 0, width, axis=dim), axis, backward)
        block = jnp.concatenate([low, block, high], axis=dim)
    return block


def prefix_2(x, axis, combine, identity, reverse):
    peers, here = (lax.axis_size(axis), lax.axis_index(axis))
    everything = jax.tree.map(lambda part: lax.all_gather(part, axis), x)
    start = jax.tree.map(
        lambda part, zero: jnp.broadcast_to(jnp.asarray(zero, part.dtype), part.shape), x, identity
    )

    def hop(k, before):
        at = peers - 1 - k if reverse else k
        reached = at > here if reverse else at < here
        new = combine(before, jax.tree.map(lambda part: part[at], everything))
        return jax.tree.map(lambda a, b: jnp.where(reached, a, b), new, before)

    return lax.fori_loop(0, peers, hop, start)


def coefficients(velocity, penalty):
    along = velocity[0]
    vertical = velocity[1]
    spanwise = velocity[2]
    west_coef = stream_coef + stream_conv * jnp.maximum(-along, 0.0)
    east_coef = stream_coef + stream_conv * jnp.maximum(along, 0.0)
    south_coef = cross_coef + cross_conv * jnp.maximum(-vertical, 0.0)
    north_coef = cross_coef + cross_conv * jnp.maximum(vertical, 0.0)
    below_coef = cross_coef + cross_conv * jnp.maximum(-spanwise, 0.0)
    above_coef = cross_coef + cross_conv * jnp.maximum(spanwise, 0.0)
    diagonal_coef = (
        west_coef
        + east_coef
        + south_coef
        + north_coef
        + below_coef
        + above_coef
        + penalty
        + shift_coef
    )
    return (west_coef, east_coef, (south_coef, north_coef, below_coef, above_coef), diagonal_coef)


def explicit_side(adjoint_source, padded, adjoint, cross):
    south_coef, north_coef, below_coef, above_coef = cross
    result = adjoint_source + shift_coef * adjoint
    result = result + south_coef * padded[:, :, 1:-1, :-2] + north_coef * padded[:, :, 1:-1, 2:]
    result = result + below_coef * padded[:, :, :-2, 1:-1] + above_coef * padded[:, :, 2:, 1:-1]
    return result


def forward(carried, row_data):
    factor, offset = carried
    lower_coef, upper_coef, pivot_base, right_row = row_data
    pivot_value = pivot_base - lower_coef * factor
    factor_next = upper_coef / pivot_value
    offset_next = (right_row + lower_coef * offset) / pivot_value
    return ((factor_next, offset_next), (factor_next, offset_next))


def compose_row(matrix, lower_norm, upper_norm, right_norm):
    first_row = upper_norm * matrix[2]
    second_row = lower_norm * matrix[1] + right_norm * matrix[2]
    third_row = matrix[2] - lower_norm * matrix[0]
    return jnp.stack([first_row, second_row, third_row])


def multiply(left_mat, right_mat):
    return jnp.sum(left_mat[:, :, None] * right_mat[None, :, :], axis=1)


def rescale(matrix):
    return matrix / jnp.max(jnp.abs(matrix), axis=(0, 1), keepdims=True)


def combine_forward(earlier, later):
    return rescale(multiply(later, earlier))


def combine_backward(earlier, later):
    return (later[0] * earlier[0], later[0] * earlier[1] + later[1])


def sweep_body(adjoint_source, adjoint, west_coef, east_coef, cross, diagonal_coef):
    padded = padded_2(adjoint, (("vert", 3), ("span", 2)), 1)
    right_side = explicit_side(adjoint_source, padded, adjoint, cross)
    rows_first = jnp.moveaxis(right_side, 1, 0)
    lower_norm = west_coef / diagonal_coef
    upper_norm = east_coef / diagonal_coef
    right_norm = rows_first / diagonal_coef[:, None]
    line_shape = rows_first.shape[1:]
    identity_mat = jnp.broadcast_to(
        jnp.eye(3, dtype=jnp.float32)[:, :, None, None, None], (3, 3) + line_shape
    )

    def chain_row(matrix, row_data):
        return (compose_row(matrix, row_data[0], row_data[1], row_data[2]), None)

    composite, unused = lax.scan(chain_row, identity_mat, (lower_norm, upper_norm, right_norm))
    composite = rescale(composite)
    prefix = prefix_2(composite, "stream", combine_forward, identity_mat, False)
    factor_in = prefix[0, 2] / prefix[2, 2]
    offset_in = prefix[1, 2] / prefix[2, 2]
    ending, (factors, offsets) = lax.scan(
        forward, (factor_in, offset_in), (west_coef, east_coef, diagonal_coef, rows_first)
    )

    def fold_back(carried, row_data):
        factor, offset = row_data
        slope_next = factor * carried[0]
        intercept_next = offset + factor * carried[1]
        return ((slope_next, intercept_next), (slope_next, intercept_next))

    ones_line = jnp.ones(line_shape, jnp.float32)
    zeros_line = jnp.zeros(line_shape, jnp.float32)
    (first_slope, first_intercept), (slopes, intercepts) = lax.scan(
        fold_back, (ones_line, zeros_line), (factors, offsets), reverse=True
    )
    incoming = prefix_2(
        (first_slope, first_intercept), "stream", combine_backward, (ones_line, zeros_line), True
    )[1]
    solved_rows = intercepts + slopes * incoming
    return jnp.moveaxis(solved_rows, 0, 1)


def shards(adjoint_source, velocity, penalty, adjoint_start, cell_band, tri_band, tri_weight):
    west_coef, east_coef, cross, diagonal_coef = coefficients(velocity, penalty)
    adjoint = adjoint_start
    for sweep_index in range(SWEEPS):
        adjoint = sweep_body(adjoint_source, adjoint, west_coef, east_coef, cross, diagonal_coef)
    sensitivity = penalty * jnp.sum(velocity * adjoint, axis=0)
    flat_band = cell_band.reshape(cell_band.shape[0], -1)
    flat_sens = sensitivity.reshape(sensitivity.shape[0], -1)
    labels = jnp.arange(NBANDS, dtype=jnp.int32)

    def add_band(running, row_data):
        onehot = (row_data[0][:, None] == labels[None, :]).astype(jnp.float32)
        return (running + jnp.dot(row_data[1], onehot, precision=lax.Precision.HIGHEST), None)

    partial_sums, unused = lax.scan(
        add_band, jnp.zeros((NBANDS,), jnp.float32), (flat_band, flat_sens)
    )
    device_count = lax.axis_size("stream") * lax.axis_size("vert") * lax.axis_size("span")
    cell_total = penalty.shape[0] * penalty.shape[1] * penalty.shape[2] * device_count
    band_scale = (NBANDS / cell_total) ** 0.5
    band_sums = lax.psum(partial_sums, ("stream", "vert", "span")) * band_scale
    onehot_tri = (tri_band[:, None] == labels[None, :]).astype(jnp.float32)
    tri_grad = tri_weight * jnp.sum(onehot_tri * band_sums[None, :], axis=1)
    return (adjoint, tri_grad)


def solution(mesh):
    return jax.shard_map(
        shards,
        mesh=mesh,
        in_specs=(
            P(None, "stream", "span", "vert"),
            P(None, "stream", "span", "vert"),
            P("stream", "span", "vert"),
            P(None, "stream", "span", "vert"),
            P("stream", "span", "vert"),
            P(("stream", "vert", "span")),
            P(("stream", "vert", "span")),
        ),
        out_specs=(P(None, "stream", "span", "vert"), P(("stream", "vert", "span"))),
        check_vma=False,
    )
```

profile of v0, /device:TPU:1, one launch (start us, length us, event | category | flops | bytes accessed | tf_op | source)
XLA Modules:
  0.0 399.3 jit_solution(9911331988854353181)
XLA Ops:
  7.2 1.1 copy.41
  8.5 4.0 collective-permute-start
  12.4 1.3 collective-permute-start.1
  16.0 3.8 collective-permute-done.1
  20.1 3.2 collective-permute-start.2
  23.3 1.3 collective-permute-start.3
  24.6 3.4 collective-permute-done.3
  28.7 1.2 while.163
  30.9 55.2 %all-gather.9.cloned.1.call-done = f32[48,3,3,12,256]{4,3,2,1,0:T(8,128)} async-done(((f32[3,3,3,12,256]{4,3,2,1,0:T(8,128)}), f32[48,3,3,12,256]{4,3,2,1,0:T(8,128)}) %all-gather.9.cloned.1.call-update) | async-done | bytes 5308432 | tf_op jit(solution)/shard_map/all_gather | solution.py:32
  86.2 22.1 %while.164 = (s32[]{:T(128)}, f32[3,3,3,12,256]{4,3,2,1,0:T(8,128)S(1)}, s32[]{:T(128)}, f32[16,3,3,3,12,256]{5,4,3,2,1,0:T(8,128)}, s32[]{:T(128)}) while((s32[]{:T(128)}, f32[3,3,3,12,256]{4,3,2,1,0:T(8,128)S(1)}, s32[]{:T(128)}, f32[16,3,3,3,12,256]{5,4,3,2,1,0:T(8,128)}, s32[]{:T(128)}) %tuple.360), condition=%wide.region_6.7_spmd, body=%wide.region_3.6_spmd.sunk | while | flops 737283 | bytes 3059787 | solution.py:43
  86.3 1.0 dynamic-slice_bitcast_fusion.26
  87.6 1.0 dynamic-slice_bitcast_fusion.26
  89.0 1.0 dynamic-slice_bitcast_fusion.26
  90.4 1.0 dynamic-slice_bitcast_fusion.26
  91.8 1.0 dynamic-slice_bitcast_fusion.26
  93.1 1.0 dynamic-slice_bitcast_fusion.26
  94.5 1.0 dynamic-slice_bitcast_fusion.26
  95.9 1.0 dynamic-slice_bitcast_fusion.26
  97.3 1.0 dynamic-slice_bitcast_fusion.26
  98.7 1.0 dynamic-slice_bitcast_fusion.26
  100.0 1.0 dynamic-slice_bitcast_fusion.26
  101.4 1.0 dynamic-slice_bitcast_fusion.26
  109.7 17.9 %all-gather.1 = f32[48,12,256]{2,1,0:T(8,128)S(1)} all-gather(f32[3,12,256]{2,1,0:T(8,128)S(1)} %get-tuple-element.895), channel_id=3, replica_groups=mesh['stream'=16,'vert'=4,'span'=4] {'stream'}, dimensions={0}, use_global_device_ids=true | all-gather | bytes 626688 | tf_op jit(solution)/shard_map/all_gather | solution.py:32
  127.5 16.9 %all-gather.2 = f32[48,12,256]{2,1,0:T(8,128)S(1)} all-gather(f32[3,12,256]{2,1,0:T(8,128)S(1)} %get-tuple-element.896), channel_id=4, replica_groups=mesh['stream'=16,'vert'=4,'span'=4] {'stream'}, dimensions={0}, use_global_device_ids=true | all-gather | bytes 626688 | tf_op jit(solution)/shard_map/all_gather | solution.py:32
  145.5 3.1 collective-permute-start.4
  148.6 1.3 collective-permute-start.5
  149.9 2.8 collective-permute-done.4
  152.7 3.8 collective-permute-done.5
  156.8 3.1 collective-permute-start.6
  159.9 1.3 collective-permute-start.7
  161.2 3.4 collective-permute-done.7
  165.3 6.9 %while.166 = (s32[]{:T(128)}, f32[3,3,3,12,256]{4,3,2,1,0:T(8,128)S(1)}, f32[8,12,256]{2,1,0:T(8,128)}, f32[8,12,256]{2,1,0:T(8,128)}, f32[8,3,12,256]{3,2,1,0:T(8,128)S(1)}, /*index=5*/s32[]{:T(128)}) while((s32[]{:T(128)}, f32[3,3,3,12,256]{4,3,2,1,0:T(8,128)S(1)}, f32[8,12,256]{2,1,0:T(8,128)}, f32[8,12,256]{2,1,0:T(8,128)}, ...), condition=%wide.region_14.15_spmd, body=%wide.region_13.14_spmd.sunk | while | flops 331778 | bytes 1511501 | solution.py:124
  173.1 51.4 %all-gather.11.cloned.1.call-done = f32[48,3,3,12,256]{4,3,2,1,0:T(8,128)} async-done(((f32[3,3,3,12,256]{4,3,2,1,0:T(8,128)}), f32[48,3,3,12,256]{4,3,2,1,0:T(8,128)}) %all-gather.11.cloned.1.call-update) | async-done | bytes 5308432 | tf_op jit(solution)/shard_map/all_gather | solution.py:32
  224.7 22.0 %while.167 = (s32[]{:T(128)}, f32[3,3,3,12,256]{4,3,2,1,0:T(8,128)S(1)}, s32[]{:T(128)}, f32[16,3,3,3,12,256]{5,4,3,2,1,0:T(8,128)}, s32[]{:T(128)}) while((s32[]{:T(128)}, f32[3,3,3,12,256]{4,3,2,1,0:T(8,128)S(1)}, s32[]{:T(128)}, f32[16,3,3,3,12,256]{5,4,3,2,1,0:T(8,128)}, s32[]{:T(128)}) %tuple.361), condition=%wide.region_19.20_spmd, body=%wide.region_16.19_spmd.sunk | while | flops 737283 | bytes 3059787 | solution.py:43
  246.8 11.9 %while.168 = (s32[]{:T(128)}, f32[3,12,256]{2,1,0:T(8,128)S(1)}, f32[3,12,256]{2,1,0:T(8,128)S(1)}, f32[8,3,12,256]{3,2,1,0:T(8,128)S(1)}, f32[8,3,12,256]{3,2,1...) while((s32[]{:T(128)}, f32[3,12,256]{2,1,0:T(8,128)S(1)}, ...), condition=%wide.region_21.22_spmd, body=%wide.region_20.21_spmd.sunk | while | flops 55298 | bytes 467057 | solution.py:129
  258.8 3.8 while.171
  262.6 17.7 %all-gather.4 = f32[48,12,256]{2,1,0:T(8,128)S(1)} all-gather(f32[3,12,256]{2,1,0:T(8,128)S(1)} %get-tuple-element.904), channel_id=6, replica_groups=mesh['stream'=16,'vert'=4,'span'=4] {'stream'}, dimensions={0}, use_global_device_ids=true | all-gather | bytes 626688 | tf_op jit(solution)/shard_map/all_gather | solution.py:32
  280.4 16.9 %all-gather.5 = f32[48,12,256]{2,1,0:T(8,128)S(1)} all-gather(f32[3,12,256]{2,1,0:T(8,128)S(1)} %get-tuple-element.905), channel_id=7, replica_groups=mesh['stream'=16,'vert'=4,'span'=4] {'stream'}, dimensions={0}, use_global_device_ids=true | all-gather | bytes 626688 | tf_op jit(solution)/shard_map/all_gather | solution.py:32
  298.9 16.4 %while.173 = (s32[]{:T(128)}, f32[256]{0:T(256)S(1)}, f32[8,3072]{1,0:T(8,128)S(1)}, s32[8,3072]{1,0:T(8,128)}, s32[]{:T(128)}, /*index=5*/s32[]{:T(128)}) while((s32[]{:T(128)}, f32[256]{0:T(256)S(1)}, f32[8,3072]{1,0:T(8,128)S(1)}, s32[8,3072]{1,0:T(8,128)}, s32[]{:T(128)}, /*index=5*/s32[]{:T(128)}) %tuple.367), condition=%wide.region_28.29_spmd.clone, body=%wide.region_27.28_spmd.clone.sunk | while | flops 10224131 | bytes 53335 | solution.py:165
  299.9 1.1 fusion.73
  301.9 1.1 fusion.73
  304.0 1.1 fusion.73
  306.0 1.1 fusion.73
  308.1 1.1 fusion.73
  310.1 1.1 fusion.73
  312.2 1.1 fusion.73
  314.2 1.1 fusion.73
  315.4 76.4 %psum.7 = f32[256]{0:T(256)S(1)} all-reduce(f32[256]{0:T(256)S(1)} %get-tuple-element.907), channel_id=1, replica_groups=mesh['stream'=16,'vert'=4,'span'=4] {'stream','vert','span'}, use_global_device_ids=true, to_apply=%region_29.30 | all-reduce | flops 256 | bytes 2048 | tf_op jit(solution)/shard_map/psum | solution.py:171
  (404 shorter events, 72.4 us)
Async XLA Ops:
  7.2 7.8 %copy-start.8 = (f32[8,12,256]{2,0,1:T(8,128)S(1)}, f32[8,12,256]{2,0,1:T(8,128)}, u32[]{:S(2)}) copy-start(f32[8,12,256]{2,0,1:T(8,128)} %param.31) | copy-start | bytes 294916
  7.2 20.8 %copy-start = (f32[3,8,12,256]{3,1,2,0:T(8,128)S(1)}, f32[3,8,12,256]{3,1,2,0:T(8,128)}, u32[]{:S(2)}) copy-start(f32[3,8,12,256]{3,1,2,0:T(8,128)} %param.29) | copy-start | bytes 884740
  7.2 78.9 %all-gather.9.cloned.1.call-start = ((), (), s32[]{:S(2)}) async-start(), calls=%async_computation | async-start | bytes 7520256 | tf_op jit(solution)/shard_map/all_gather | solution.py:32
  8.5 7.5 %collective-permute-start = (f32[3,8,12,1]{3,2,0,1:T(8,128)S(1)}, f32[3,8,12,1]{3,2,0,1:T(8,128)S(1)}, u32[]{:S(2)}, u32[]{:S(2)}) collective-permute-start(f32[3,8,12,1]{3,2,0,1:T(8,128)S(1)} %get-tuple-element.1189), channel_id=1, source_target_pairs={{0,4},{4,8},{8,12},{1,5},{5,9},{9,13},{2,6},{6,10},{10,14},{3,7},{... | collective-permute-start | bytes 3464 | tf_op jit(solution)/shard_map/ppermute | solution.py:22
  12.4 7.3 %collective-permute-start.1 = (f32[3,8,12,1]{3,2,0,1:T(8,128)S(1)}, f32[3,8,12,1]{3,2,0,1:T(8,128)S(1)}, u32[]{:S(2)}, u32[]{:S(2)}) collective-permute-start(f32[3,8,12,1]{3,2,0,1:T(8,128)S(1)} %get-tuple-element.1190), channel_id=1, source_target_pairs={{4,0},{8,4},{12,8},{5,1},{9,5},{13,9},{6,2},{10,6},{14,10},{7,3},{... | collective-permute-start | bytes 3464 | tf_op jit(solution)/shard_map/ppermute | solution.py:25
  14.8 13.8 %copy-start.1 = (f32[8,12,256]{2,1,0:T(8,128)}, f32[8,12,256]{2,1,0:T(8,128)S(1)}, u32[]{:S(2)}) copy-start(f32[8,12,256]{2,1,0:T(8,128)S(1)} %get-tuple-element.1198) | copy-start | bytes 294916
  20.1 4.5 %collective-permute-start.2 = (f32[3,8,1,258]{3,2,0,1:T(1,128)S(1)}, f32[3,8,1,258]{3,2,0,1:T(1,128)S(1)}, u32[]{:S(2)}, u32[]{:S(2)}) collective-permute-start(f32[3,8,1,258]{3,2,0,1:T(1,128)S(1)} %get-tuple-element.1181), channel_id=1, source_target_pairs={{0,1},{1,2},{2,3},{4,5},{5,6},{6,7},{8,9},{9,10},{10,11},{12,13},{... | collective-permute-start | bytes 74312 | tf_op jit(solution)/shard_map/ppermute | solution.py:22
  23.3 4.7 %collective-permute-start.3 = (f32[3,8,1,258]{3,2,0,1:T(1,128)S(1)}, f32[3,8,1,258]{3,2,0,1:T(1,128)S(1)}, u32[]{:S(2)}, u32[]{:S(2)}) collective-permute-start(f32[3,8,1,258]{3,2,0,1:T(1,128)S(1)} %get-tuple-element.1182), channel_id=1, source_target_pairs={{1,0},{2,1},{3,2},{5,4},{6,5},{7,6},{9,8},{10,9},{11,10},{13,12},{... | collective-permute-start | bytes 74312 | tf_op jit(solution)/shard_map/ppermute | solution.py:25
  24.6 61.5 %copy-start.9 = (f32[3,3]{1,0:T(4,128)}, f32[3,3]{1,0:T(4,128)S(1)}, u32[]{:S(2)}) copy-start(f32[3,3]{1,0:T(4,128)S(1)} %fusion.53) | copy-start | bytes 112
  29.9 56.3 %copy-start.4 = (f32[8,12,256]{2,1,0:T(8,128)}, f32[8,12,256]{2,1,0:T(8,128)S(1)}, u32[]{:S(2)}) copy-start(f32[8,12,256]{2,1,0:T(8,128)S(1)} %get-tuple-element.1924) | copy-start | bytes 294916
  29.9 56.3 %copy-start.7 = (f32[8,12,256]{2,1,0:T(8,128)}, f32[8,12,256]{2,1,0:T(8,128)S(1)}, u32[]{:S(2)}) copy-start(f32[8,12,256]{2,1,0:T(8,128)S(1)} %get-tuple-element.1927) | copy-start | bytes 294916
  30.8 193.7 %all-gather.11.cloned.1.call-start = ((), (), s32[]{:S(2)}) async-start(), calls=%async_computation.1 | async-start | bytes 7520256 | tf_op jit(solution)/shard_map/all_gather | solution.py:32
  109.1 18.4 %copy-start.5 = (f32[8,12,256]{2,1,0:T(8,128)}, f32[8,12,256]{2,1,0:T(8,128)S(1)}, u32[]{:S(2)}) copy-start(f32[8,12,256]{2,1,0:T(8,128)S(1)} %get-tuple-element.1925) | copy-start | bytes 294916
  109.1 18.4 %copy-start.6 = (f32[8,12,256]{2,1,0:T(8,128)}, f32[8,12,256]{2,1,0:T(8,128)S(1)}, u32[]{:S(2)}) copy-start(f32[8,12,256]{2,1,0:T(8,128)S(1)} %get-tuple-element.1926) | copy-start | bytes 294916
  109.6 54.9 %copy-start.2 = (f32[8,12,256]{2,1,0:T(8,128)S(1)}, f32[8,12,256]{2,1,0:T(8,128)}, u32[]{:S(2)}) copy-start(f32[8,12,256]{2,1,0:T(8,128)} %copy-done.1) | copy-start | bytes 294916
  145.3 19.9 %copy-start.10 = (f32[3,3]{1,0:T(4,128)S(1)}, f32[3,3]{1,0:T(4,128)}, u32[]{:S(2)}) copy-start(f32[3,3]{1,0:T(4,128)} %copy-done.9) | copy-start | bytes 112
  145.5 7.2 %collective-permute-start.4 = (f32[3,8,12,1]{3,2,0,1:T(8,128)S(1)}, f32[3,8,12,1]{3,2,0,1:T(8,128)S(1)}, u32[]{:S(2)}, u32[]{:S(2)}) collective-permute-start(f32[3,8,12,1]{3,2,0,1:T(8,128)S(1)} %get-tuple-element.1187), channel_id=1, source_target_pairs={{0,4},{4,8},{8,12},{1,5},{5,9},{9,13},{2,6},{6,10},{10,14},{3,7},{... | collective-permute-start | bytes 3464 | tf_op jit(solution)/shard_map/ppermute | solution.py:22
  148.6 7.9 %collective-permute-start.5 = (f32[3,8,12,1]{3,2,0,1:T(8,128)S(1)}, f32[3,8,12,1]{3,2,0,1:T(8,128)S(1)}, u32[]{:S(2)}, u32[]{:S(2)}) collective-permute-start(f32[3,8,12,1]{3,2,0,1:T(8,128)S(1)} %get-tuple-element.1188), channel_id=1, source_target_pairs={{4,0},{8,4},{12,8},{5,1},{9,5},{13,9},{6,2},{10,6},{14,10},{7,3},{... | collective-permute-start | bytes 3464 | tf_op jit(solution)/shard_map/ppermute | solution.py:25
  156.8 4.4 %collective-permute-start.6 = (f32[3,8,1,258]{3,2,0,1:T(1,128)S(1)}, f32[3,8,1,258]{3,2,0,1:T(1,128)S(1)}, u32[]{:S(2)}, u32[]{:S(2)}) collective-permute-start(f32[3,8,1,258]{3,2,0,1:T(1,128)S(1)} %get-tuple-element.1179), channel_id=1, source_target_pairs={{0,1},{1,2},{2,3},{4,5},{5,6},{6,7},{8,9},{9,10},{10,11},{12,13},{... | collective-permute-start | bytes 74312 | tf_op jit(solution)/shard_map/ppermute | solution.py:22
  159.9 4.7 %collective-permute-start.7 = (f32[3,8,1,258]{3,2,0,1:T(1,128)S(1)}, f32[3,8,1,258]{3,2,0,1:T(1,128)S(1)}, u32[]{:S(2)}, u32[]{:S(2)}) collective-permute-start(f32[3,8,1,258]{3,2,0,1:T(1,128)S(1)} %get-tuple-element.1180), channel_id=1, source_target_pairs={{1,0},{2,1},{3,2},{5,4},{6,5},{7,6},{9,8},{10,9},{11,10},{13,12},{... | collective-permute-start | bytes 74312 | tf_op jit(solution)/shard_map/ppermute | solution.py:25
  258.8 39.4 %copy-start.3 = (f32[3,8,12,256]{3,1,2,0:T(8,128)S(1)}, f32[3,8,12,256]{3,1,2,0:T(8,128)}, u32[]{:S(2)}) copy-start(f32[3,8,12,256]{3,1,2,0:T(8,128)} %param.30) | copy-start | bytes 884740
  298.1 93.7 %copy-start.11 = (s32[128]{0:T(128)S(1)}, s32[128]{0:T(128)}, u32[]{:S(2)}) copy-start(s32[128]{0:T(128)} %param.34) | copy-start | bytes 1540
  298.1 93.8 %copy-start.12 = (f32[128]{0:T(128)S(1)}, f32[128]{0:T(128)}, u32[]{:S(2)}) copy-start(f32[128]{0:T(128)} %param.35) | copy-start | bytes 1540
Sparse Core Ops, SparseCore 0:
  30.9 55.1 all-gather.8
  173.2 51.2 all-gather.10
where the time goes:
time: 403 us; the launch traced here: 399 us
  blocking collectives  146 us (36%)
  waiting for transfers between devices  125 us (31%)
  local copies, waits for them, and re-layouts  64.9 us (16%)
  starting transfers between devices  18.6 us (5%)
  other arithmetic  17.6 us (4%)
  between operations  14.6 us (4%)
  matrix products  8.88 us (2%)
  loops' own time  4.2 us (1%)
    all_gather x2, waiting for transfers between devices, prefix_2(): everything = jax.tree.map(lambda part: lax.all_gather(part, axis), x)  107 us
    psum x1, blocking collectives, shards(): band_sums = lax.psum(partial_sums, ('stream', 'vert', 'span')) * band_scale  76.4 us
    all_gather x4, blocking collectives, prefix_2(): everything = jax.tree.map(lambda part: lax.all_gather(part, axis), x)  69.5 us
    mul x32, local copies, waits for them, and re-layouts, multiply(): return jnp.sum(left_mat[:, :, None] * right_mat[None, :, :], axis=1)  33.5 us
    ppermute x4, waiting for transfers between devices, padded_2(): lax.ppermute(lax.slice_in_dim(block, 0, width, axis=dim), axis, backward)  14.4 us
    ppermute x4, starting transfers between devices, padded_2(): lax.ppermute(lax.slice_in_dim(block, block.shape[dim] - width, None, axis...  13.4 us
    dot_general x8, matrix products, add_band(): jnp.dot(row_data[1], onehot, precision=lax.Precision.HIGHEST)  8.88 us
  transfers between devices with their start and end apart: 10, of which 8 were waited for; matrix products, arithmetic and copies ran while one was open for 0% of the time, Pallas kernels for 0%

commit v1 on v0

v1 whole, which is shorter than its diff:
```python
import functools

import jax
import jax.numpy as jnp
from jax import lax
from jax.experimental import pallas as pl
from jax.experimental.pallas import tpu as pltpu
from jax.sharding import PartitionSpec as P

SWEEPS = 2
NBANDS = 256

STREAM = 16
VERT = 4
SPAN = 4
NC = 3
NXL = 8
NZL = 12
NYL = 256
ZP = 16
LANES = 128

stream_coef = 1000.0
stream_conv = 200.0
cross_coef = 0.25
cross_conv = 0.25
shift_coef = 0.5

MESH = pl.DeviceIdType.MESH
F32 = jnp.float32


OWNERS = 9


def owner_of(o):
    return jnp.where(o == OWNERS - 1, 9, 2 * o)


def kernel(
    src_h,
    vel_h,
    pen_h,
    start_h,
    band_h,
    tb_ref,
    tw_ref,
    out_h,
    tri_ref,
    SRC_IN,
    VEL,
    PEN,
    BAND,
    START,
    SRC,
    A1,
    A2,
    A3,
    PO,
    CR,
    IP,
    MM,
    FF,
    LL,
    RC,
    YS,
    YR,
    ZS,
    ZR,
    MS,
    MR,
    PS,
    PR,
    RS,
    RR,
    CO,
    OC,
    SH,
    SL,
    OHB,
    B1S,
    B1R,
    B2S,
    B2R,
    in_sem,
    out_sem,
    halo_send,
    halo_recv,
    m_send,
    m_recv,
    p_send,
    p_recv,
    r_send,
    r_recv,
    b_send,
    b_recv,
):
    me = lax.axis_index("stream")
    mv = lax.axis_index("vert")
    mp = lax.axis_index("span")

    def local_in(k, src, dst):
        return pltpu.make_async_copy(src, dst, in_sem.at[k])

    in_start = local_in(0, start_h, START)
    in_vel = local_in(1, vel_h, VEL)
    in_pen = local_in(2, pen_h, PEN)
    in_src = local_in(3, src_h, SRC_IN)
    in_band = local_in(4, band_h, BAND)
    for c in (in_start, in_vel, in_pen, in_src, in_band):
        c.start()

    YR[...] = jnp.zeros(YR.shape, F32)
    ZR[...] = jnp.zeros(ZR.shape, F32)

    barrier = pltpu.get_barrier_semaphore()

    def greet(j, carry):
        pl.semaphore_signal(
            barrier, inc=1, device_id=(lax.rem(me + j, STREAM), mv, mp), device_id_type=MESH
        )
        pl.semaphore_signal(
            barrier,
            inc=1,
            device_id=(me, lax.rem(mv + j // SPAN, VERT), lax.rem(mp + j % SPAN, SPAN)),
            device_id_type=MESH,
        )
        return carry

    lax.fori_loop(1, STREAM, greet, 0)

    lane = lax.broadcasted_iota(jnp.int32, (ZP, LANES), 1)

    def half(ref, c, x, t):
        return ref[c, x, :, t * LANES : (t + 1) * LANES]

    def pack_edges(k, a0, a1, low, high):
        low = jnp.where(lane == k, pltpu.roll(a0, k, 1), low)
        high = jnp.where(lane == k, pltpu.roll(a1, k + 1, 1), high)
        return low, high

    def halo_copies(s):
        def remote(i, src, dst, v, p):
            return pltpu.make_async_remote_copy(
                src_ref=src,
                dst_ref=dst,
                send_sem=halo_send.at[s, i],
                recv_sem=halo_recv.at[s, i],
                device_id=(me, v, p),
                device_id_type=MESH,
            )

        up = remote(0, ZS.at[s, 1], ZR.at[s, 0], mv, lax.rem(mp + 1, SPAN))
        down = remote(1, ZS.at[s, 0], ZR.at[s, 1], mv, lax.rem(mp + SPAN - 1, SPAN))
        north = remote(2, YS.at[s, 1], YR.at[s, 0], lax.rem(mv + 1, VERT), mp)
        south = remote(3, YS.at[s, 0], YR.at[s, 1], lax.rem(mv + VERT - 1, VERT), mp)
        return (
            (up, mp < SPAN - 1, mp > 0),
            (down, mp > 0, mp < SPAN - 1),
            (north, mv < VERT - 1, mv > 0),
            (south, mv > 0, mv < VERT - 1),
        )

    def each(copies, which, act):
        for item in copies:
            pl.when(item[which])(functools.partial(act, item[0]))

    def to_owners(src_of, dst, send_sem, recv_sem):
        def send(o, carry):
            owner = owner_of(o)

            @pl.when(owner != me)
            def _():
                pltpu.make_async_remote_copy(
                    src_ref=src_of(o),
                    dst_ref=dst,
                    send_sem=send_sem,
                    recv_sem=recv_sem,
                    device_id=(owner, mv, mp),
                    device_id_type=MESH,
                ).start()

            @pl.when(owner == me)
            def _():
                pltpu.make_async_copy(src_of(o), dst, recv_sem).start()

            return carry

        lax.fori_loop(0, OWNERS, send, 0)

    def drain(count, ref, sem):
        def one(j, carry):
            pltpu.make_async_copy(ref, ref, sem).wait()
            return carry

        lax.fori_loop(0, count, one, 0)

    is_owner = jnp.logical_or(lax.rem(me, 2) == 0, me == 9)
    my_o = jnp.where(me == 9, OWNERS - 1, me // 2)
    owner_sends = jnp.where(is_owner, OWNERS - 1, OWNERS)

    in_start.wait()
    zero_tile = jnp.zeros((ZP, LANES), F32)

    def pack_start(x, carry):
        low, high = carry
        for c in range(NC):
            k = c * NXL + x
            A1[c, x, 0:NZL, :] = START[c, x]
            ZS[0, 0, k] = START[c, x, 0:1, :]
            ZS[0, 1, k] = START[c, x, NZL - 1 : NZL, :]
            low, high = pack_edges(k, half(A1, c, x, 0), half(A1, c, x, 1), low, high)
        return low, high

    low, high = lax.fori_loop(0, NXL, pack_start, (zero_tile, zero_tile))
    YS[0, 0] = low
    YS[0, 1] = high

    pl.semaphore_wait(barrier, 2 * (STREAM - 1))
    halo1 = halo_copies(0)
    each(halo1, 1, lambda c: c.start())

    in_vel.wait()
    in_pen.wait()

    ones = jnp.ones((NZL, NYL), F32)

    def factor(x, carry):
        delta, lam = carry
        u = VEL[0, x]
        v = VEL[1, x]
        w = VEL[2, x]
        west = stream_coef + stream_conv * jnp.maximum(-u, 0.0)
        east = stream_coef + stream_conv * jnp.maximum(u, 0.0)
        CR[0, x, 0:NZL, :] = cross_coef + cross_conv * jnp.maximum(-v, 0.0)
        CR[1, x, 0:NZL, :] = cross_coef + cross_conv * jnp.maximum(v, 0.0)
        CR[2, x, 0:NZL, :] = cross_coef + cross_conv * jnp.maximum(-w, 0.0)
        CR[3, x, 0:NZL, :] = cross_coef + cross_conv * jnp.maximum(w, 0.0)
        excess = (
            (4.0 * cross_coef + shift_coef) + cross_conv * (jnp.abs(v) + jnp.abs(w)) + PEN[x]
        )
        ip = 1.0 / (east + (excess + west * delta))
        m = west * ip
        IP[x, 0:NZL, :] = ip
        MM[x, 0:NZL, :] = m
        FF[x, 0:NZL, :] = east * ip
        lam = m * lam
        LL[x, 0:NZL, :] = lam
        return (excess + west * delta) * ip, lam

    delta, lam = lax.fori_loop(0, NXL, factor, (ones, ones))
    l_last = LL[NXL - 1]
    r_last = FF[NXL - 1]
    RC[NXL - 1] = r_last

    def fold(i, carry):
        l, r = carry
        x = NXL - 2 - i
        f = FF[x]
        l = LL[x] + f * l
        r = f * r
        LL[x] = l
        RC[x] = r
        return l, r

    l_first, r_first = lax.fori_loop(0, NXL - 1, fold, (l_last, r_last))
    for k, value in enumerate((l_first, l_last, r_first, r_last)):
        for t in range(2):
            cut = slice(t * LANES, (t + 1) * LANES)
            MS[t, 8 * k : 8 * k + 8, :] = value[0:8, cut]
            MS[2, 8 * k + 4 * t : 8 * k + 4 * t + 4, :] = value[8:NZL, cut]
    to_owners(lambda o: MS.at[o // NC], MR.at[me], m_send, m_recv)

    in_band.wait()
    iota_l = lax.broadcasted_iota(jnp.int32, (16, NYL), 0)

    def onehot(x, carry):
        for z in range(NZL):
            low_part = lax.rem(BAND[x, z : z + 1, :], 16)
            OHB[x, :, z * NYL : (z + 1) * NYL] = jnp.where(
                jnp.broadcast_to(low_part, (16, NYL)) == iota_l, 1.0, 0.0
            ).astype(jnp.bfloat16)
        return carry

    lax.fori_loop(0, NXL, onehot, 0)

    drain(owner_sends, MS.at[0], m_send)

    @pl.when(is_owner)
    def _():
        pltpu.make_async_copy(MR, MR, m_recv).wait()

        def reduced(d, F):
            lf, lg, rf, rg = (MR[d, 8 * k : 8 * k + 8, :] for k in range(4))
            inv = 1.0 / (1.0 - lf * F)
            b = lg * inv
            g = b * F
            CO[d, 0] = g
            CO[d, 1] = b
            CO[d, 2] = inv
            CO[d, 3] = lf * inv
            CO[d, 4] = rf * inv
            CO[d, 5] = F
            return rg + g * rf

        lax.fori_loop(0, STREAM, reduced, jnp.zeros((8, LANES), F32))

    in_src.wait()

    def pad_source(x, carry):
        for c in range(NC):
            SRC[c, x, 0:NZL, :] = SRC_IN[c, x]
        return carry

    lax.fori_loop(0, NXL, pad_source, 0)
    first = lane == 0
    last = lane == LANES - 1
    depth = lax.broadcasted_iota(jnp.int32, (ZP, LANES), 0)
    floor = depth == 0
    top = depth == NZL - 1

    def sweep(s, A, halo, store):
        each(halo, 2, lambda c: c.wait_recv())
        hl = YR[s, 0]
        hh = YR[s, 1]

        def row(x, offsets):
            south, north, below, above = (CR[i, x] for i in range(4))
            ip = IP[x]
            m = MM[x]
            new = []
            for c in range(NC):
                k = c * NXL + x
                a0 = half(A, c, x, 0)
                a1 = half(A, c, x, 1)
                r0 = pltpu.roll(a0, 1, 1)
                r1 = pltpu.roll(a1, 1, 1)
                q0 = pltpu.roll(a0, LANES - 1, 1)
                q1 = pltpu.roll(a1, LANES - 1, 1)
                lo = pltpu.roll(hl, lax.rem(LANES - k, LANES), 1)
                hi = pltpu.roll(hh, LANES - 1 - k, 1)
                y_lo = (jnp.where(first, lo, r0), jnp.where(first, r0, r1))
                y_hi = (jnp.where(last, q1, q0), jnp.where(last, hi, q1))
                for t, a in enumerate((a0, a1)):
                    cut = slice(t * LANES, (t + 1) * LANES)
                    rhs = half(SRC, c, x, t) + shift_coef * a
                    rhs = rhs + south[:, cut] * y_lo[t] + north[:, cut] * y_hi[t]
                    z_lo = jnp.where(floor, ZR[s, 0, k, :, cut], pltpu.roll(a, 1, 0))
                    z_hi = jnp.where(top, ZR[s, 1, k, :, cut], pltpu.roll(a, ZP - 1, 0))
                    rhs = rhs + below[:, cut] * z_lo + above[:, cut] * z_hi
                    o = rhs * ip[:, cut] + m[:, cut] * offsets[2 * c + t]
                    PO[c, x, :, cut] = o
                    new.append(o)
            return tuple(new)

        o_last = lax.fori_loop(0, NXL, row, (zero_tile,) * 6)

        def back(i, p):
            x = NXL - 2 - i
            f = FF[x]
            new = []
            for c in range(NC):
                for t in range(2):
                    cut = slice(t * LANES, (t + 1) * LANES)
                    value = PO[c, x, :, cut] + f[:, cut] * p[2 * c + t]
                    PO[c, x, :, cut] = value
                    new.append(value)
            return tuple(new)

        p_first = lax.fori_loop(0, NXL - 1, back, o_last)
        for c in range(NC):
            for t in range(2):
                for place, value in ((0, p_first[2 * c + t]), (8, o_last[2 * c + t])):
                    PS[s, NC * t + c, place : place + 8, :] = value[0:8]
                    PS[s, 2 * NC + c, place + 4 * t : place + 4 * t + 4, :] = value[8:NZL]
        to_owners(lambda o: PS.at[s, o], PR.at[s, me], p_send.at[s], p_recv.at[s])

        @pl.when(is_owner)
        def _():
            everything = PR.at[s]
            pltpu.make_async_copy(everything, everything, p_recv.at[s]).wait()
            O = jnp.zeros((8, LANES), F32)
            for d in range(STREAM):
                OC[d] = O
                O = PR[s, d, 8:16, :] + CO[d, 0] * PR[s, d, 0:8, :] + CO[d, 1] * O
            f_next = jnp.zeros((8, LANES), F32)
            for d in reversed(range(STREAM)):
                RS[s, d, 8:16, :] = f_next
                O = OC[d]
                f_next = CO[d, 2] * PR[s, d, 0:8, :] + CO[d, 3] * O + CO[d, 4] * f_next
                RS[s, d, 0:8, :] = CO[d, 5] * f_next + O

            def reply(j, carry):
                d = lax.rem(me + j, STREAM)

                pltpu.make_async_remote_copy(
                    src_ref=RS.at[s, d],
                    dst_ref=RR.at[s, my_o, pl.ds(0, ZP), :],
                    send_sem=r_send.at[s],
                    recv_sem=r_recv.at[s],
                    device_id=(d, mv, mp),
                    device_id_type=MESH,
                ).start()
                return carry

            lax.fori_loop(1, STREAM, reply, 0)
            pltpu.make_async_copy(
                RS.at[s, me], RR.at[s, my_o, pl.ds(0, ZP), :], r_recv.at[s]
            ).start()

        drain(owner_sends, PS.at[s, 0], p_send.at[s])
        arrived = RR.at[s, :, pl.ds(0, ZP), :]
        pltpu.make_async_copy(arrived, arrived, r_recv.at[s]).wait()

        def interface(place):
            return [
                jnp.concatenate(
                    [
                        RR[s, NC * t + c, place : place + 8, :],
                        RR[s, 2 * NC + c, place + 4 * t : place + 4 * t + 8, :],
                    ],
                    axis=0,
                )
                for c in range(NC)
                for t in range(2)
            ]

        a_left = interface(0)
        a_right = interface(8)

        def solved(x, c, t):
            cut = slice(t * LANES, (t + 1) * LANES)
            return (
                PO[c, x, :, cut]
                + LL[x, :, cut] * a_left[2 * c + t]
                + RC[x, :, cut] * a_right[2 * c + t]
            )

        return store(solved)

    def store_first(solved):
        def line(x, carry):
            low, high = carry
            for c in range(NC):
                pair = [solved(x, c, t) for t in range(2)]
                for t in range(2):
                    A2[c, x, 0:NZL, t * LANES : (t + 1) * LANES] = pair[t][0:NZL]
                    ZS[1, 0, c * NXL + x, :, t * LANES : (t + 1) * LANES] = pair[t][0:1]
                    ZS[1, 1, c * NXL + x, :, t * LANES : (t + 1) * LANES] = pair[t][
                        NZL - 1 : NZL
                    ]
                low, high = pack_edges(c * NXL + x, pair[0], pair[1], low, high)
            return low, high

        low, high = lax.fori_loop(0, NXL, line, (zero_tile, zero_tile))
        YS[1, 0] = low
        YS[1, 1] = high

    sweep(0, A1, halo1, store_first)
    halo2 = halo_copies(1)
    each(halo2, 1, lambda c: c.start())

    def store_last(solved):
        def line(x, carry):
            for t in range(2):
                cut = slice(t * LANES, (t + 1) * LANES)
                total = None
                for c in range(NC):
                    a = solved(x, c, t)[0:NZL]
                    A3[c, x, :, cut] = a
                    term = half(VEL, c, x, t) * a
                    total = term if total is None else total + term
                total = total * PEN[x, :, cut]
                coarse = total.astype(jnp.bfloat16).astype(F32)
                SH[x, :, cut] = coarse
                SL[x, :, cut] = total - coarse
            return carry

        lax.fori_loop(0, NXL, line, 0)

    sweep(1, A2, halo2, store_last)
    out_copy = pltpu.make_async_copy(A3, out_h, out_sem)
    out_copy.start()

    def band_rows(x, acc):
        parts = []
        for z in range(NZL):
            high_part = jnp.broadcast_to(BAND[x, z : z + 1, :] // 16, (16, NYL)) == iota_l
            parts.append(
                jnp.concatenate(
                    [
                        jnp.where(high_part, jnp.broadcast_to(S[x, z : z + 1, :], (16, NYL)), 0.0)
                        for S in (SH, SL)
                    ],
                    axis=0,
                ).astype(jnp.bfloat16)
            )
        weights = jnp.concatenate(parts, axis=1)
        return acc + lax.dot_general(
            weights, OHB[x], (((1,), (1,)), ((), ())), preferred_element_type=F32
        )

    acc = lax.fori_loop(0, NXL, band_rows, jnp.zeros((32, 16), F32))
    sums = acc[0:16] + acc[16:32]
    wide = jnp.concatenate([sums] * 8, axis=1)
    keep = lax.broadcasted_iota(jnp.int32, (8, LANES), 1) // 16 == lax.broadcasted_iota(
        jnp.int32, (8, LANES), 0
    )
    for h in range(2):
        B1S[h : h + 1, :] = jnp.sum(
            jnp.where(keep, wide[8 * h : 8 * h + 8], 0.0), axis=0, keepdims=True
        )

    def band_round(r, own, slots, device_of):
        def send(j, carry):
            pltpu.make_async_remote_copy(
                src_ref=own,
                dst_ref=slots.at[j],
                send_sem=b_send.at[r],
                recv_sem=b_recv.at[r],
                device_id=device_of(j),
                device_id_type=MESH,
            ).start()
            return carry

        lax.fori_loop(1, STREAM, send, 0)
        got = slots.at[pl.ds(1, STREAM - 1)]
        pltpu.make_async_copy(got, got, b_recv.at[r]).wait()
        total = own[...]
        for j in range(1, STREAM):
            total = total + slots[j]
        return total

    B2S[...] = band_round(
        0, B1S, B1R, lambda j: (lax.rem(me + j, STREAM), mv, mp)
    )
    bands = band_round(
        1,
        B2S,
        B2R,
        lambda j: (me, lax.rem(mv + j // SPAN, VERT), lax.rem(mp + j % SPAN, SPAN)),
    )
    cells = STREAM * VERT * SPAN * NXL * NZL * NYL
    bands = bands * ((NBANDS / cells) ** 0.5)
    tb = tb_ref[...].reshape(1, LANES)
    spot = jnp.broadcast_to(lax.rem(tb, LANES), (8, LANES))
    low_half = jnp.take_along_axis(jnp.broadcast_to(bands[0:1], (8, LANES)), spot, axis=1)
    high_half = jnp.take_along_axis(jnp.broadcast_to(bands[1:2], (8, LANES)), spot, axis=1)
    picked = jnp.where(tb < LANES, low_half[0:1], high_half[0:1])
    tri_ref[...] = (tw_ref[...].reshape(1, LANES) * picked).reshape(LANES)

    out_copy.wait()
    each(halo1, 1, lambda c: c.wait_send())
    each(halo2, 1, lambda c: c.wait_send())

    @pl.when(is_owner)
    def _():
        for s in range(SWEEPS):
            drain(STREAM - 1, RS.at[s, 0], r_send.at[s])

    for r, own in enumerate((B1S, B2S)):
        drain(STREAM - 1, own, b_send.at[r])


def shards(adjoint_source, velocity, penalty, adjoint_start, cell_band, tri_band, tri_weight):
    anywhere = pl.BlockSpec(memory_space=pl.ANY)
    vmem = pl.BlockSpec(memory_space=pltpu.VMEM)
    scratch = [
        pltpu.VMEM((NC, NXL, NZL, NYL), F32),
        pltpu.VMEM((NC, NXL, NZL, NYL), F32),
        pltpu.VMEM((NXL, NZL, NYL), F32),
        pltpu.VMEM((NXL, NZL, NYL), jnp.int32),
        pltpu.VMEM((NC, NXL, NZL, NYL), F32),
        pltpu.VMEM((NC, NXL, ZP, NYL), F32),
        pltpu.VMEM((NC, NXL, ZP, NYL), F32),
        pltpu.VMEM((NC, NXL, ZP, NYL), F32),
        pltpu.VMEM((NC, NXL, NZL, NYL), F32),
        pltpu.VMEM((NC, NXL, ZP, NYL), F32),
        pltpu.VMEM((4, NXL, ZP, NYL), F32),
        pltpu.VMEM((NXL, ZP, NYL), F32),
        pltpu.VMEM((NXL, ZP, NYL), F32),
        pltpu.VMEM((NXL, ZP, NYL), F32),
        pltpu.VMEM((NXL, ZP, NYL), F32),
        pltpu.VMEM((NXL, ZP, NYL), F32),
        pltpu.VMEM((SWEEPS, 2, ZP, LANES), F32),
        pltpu.VMEM((SWEEPS, 2, ZP, LANES), F32),
        pltpu.VMEM((SWEEPS, 2, NC * NXL, 1, NYL), F32),
        pltpu.VMEM((SWEEPS, 2, NC * NXL, 1, NYL), F32),
        pltpu.VMEM((3, 32, LANES), F32),
        pltpu.VMEM((STREAM, 32, LANES), F32),
        pltpu.VMEM((SWEEPS, OWNERS, ZP, LANES), F32),
        pltpu.VMEM((SWEEPS, STREAM, ZP, LANES), F32),
        pltpu.VMEM((SWEEPS, STREAM, ZP, LANES), F32),
        pltpu.VMEM((SWEEPS, OWNERS, ZP + 8, LANES), F32),
        pltpu.VMEM((STREAM, 6, 8, LANES), F32),
        pltpu.VMEM((STREAM, 8, LANES), F32),
        pltpu.VMEM((NXL, NZL, NYL), F32),
        pltpu.VMEM((NXL, NZL, NYL), F32),
        pltpu.VMEM((NXL, 16, NZL * NYL), jnp.bfloat16),
        pltpu.VMEM((2, LANES), F32),
        pltpu.VMEM((STREAM, 2, LANES), F32),
        pltpu.VMEM((2, LANES), F32),
        pltpu.VMEM((STREAM, 2, LANES), F32),
        pltpu.SemaphoreType.DMA((5,)),
        pltpu.SemaphoreType.DMA,
        pltpu.SemaphoreType.DMA((SWEEPS, 4)),
        pltpu.SemaphoreType.DMA((SWEEPS, 4)),
        pltpu.SemaphoreType.DMA,
        pltpu.SemaphoreType.DMA,
        pltpu.SemaphoreType.DMA((SWEEPS,)),
        pltpu.SemaphoreType.DMA((SWEEPS,)),
        pltpu.SemaphoreType.DMA((SWEEPS,)),
        pltpu.SemaphoreType.DMA((SWEEPS,)),
        pltpu.SemaphoreType.DMA((2,)),
        pltpu.SemaphoreType.DMA((2,)),
    ]
    return pl.pallas_call(
        kernel,
        out_shape=(
            jax.ShapeDtypeStruct((NC, NXL, NZL, NYL), F32),
            jax.ShapeDtypeStruct((LANES,), F32),
        ),
        in_specs=[anywhere] * 5 + [vmem] * 2,
        out_specs=(anywhere, vmem),
        scratch_shapes=scratch,
        compiler_params=pltpu.CompilerParams(
            collective_id=0, has_side_effects=True, vmem_limit_bytes=32 * 1024 * 1024
        ),
    )(adjoint_source, velocity, penalty, adjoint_start, cell_band, tri_band, tri_weight)


def solution(mesh):
    return jax.shard_map(
        shards,
        mesh=mesh,
        in_specs=(
            P(None, "stream", "span", "vert"),
            P(None, "stream", "span", "vert"),
            P("stream", "span", "vert"),
            P(None, "stream", "span", "vert"),
            P("stream", "span", "vert"),
            P(("stream", "vert", "span")),
            P(("stream", "vert", "span")),
        ),
        out_specs=(P(None, "stream", "span", "vert"), P(("stream", "vert", "span"))),
        check_vma=False,
    )
```

time: 403 us -> 62.9 us (0.16)
  blocking collectives: 146 us -> 0 us
  waiting for transfers between devices: 125 us -> 0 us
  local copies, waits for them, and re-layouts: 64.9 us -> 5 us
  Pallas kernels: 0 us -> 57 us
  starting transfers between devices: 18.6 us -> 0 us
  other arithmetic: 17.6 us -> 0 us
  between operations: 14.6 us -> 0.7 us
  matrix products: 8.88 us -> 0 us
  loops' own time: 4.2 us -> 0 us
    all_gather x2 -> x0, waiting for transfers between devices: 107 us -> none  [prefix_2(): everything = jax.tree.map(lambda part: lax.all_gather(part, axis), x)]
    psum x1 -> x0, blocking collectives: 76.4 us -> none  [shards(): band_sums = lax.psum(partial_sums, ('stream', 'vert', 'span')) * band_scale]
    all_gather x4 -> x0, blocking collectives: 69.5 us -> none  [prefix_2(): everything = jax.tree.map(lambda part: lax.all_gather(part, axis), x)]
    pallas_call x0 -> x1, Pallas kernels: none -> 57 us  [shards(): pl.pallas_call(kernel, out_shape=(jax.ShapeDtypeStruct((NC, NXL, NZL, NYL...]
    mul x80 -> x0, local copies, waits for them, and re-layouts: 45.5 us -> none  [the longest x32 33.5 us: multiply(): return jnp.sum(left_mat[:, :, None] * right_mat[None, :, :], axis=1)]
    ppermute x8 -> x0, starting transfers between devices: 18.5 us -> none  [the longest x4 13.4 us: padded_2(): lax.ppermute(lax.slice_in_dim(block, block.shape[dim] - width, None, axis...]
    ppermute x8 -> x0, waiting for transfers between devices: 17.9 us -> none  [the longest x4 14.4 us: padded_2(): lax.ppermute(lax.slice_in_dim(block, 0, width, axis=dim), axis, backward)]
    dot_general x8 -> x0, matrix products: 8.88 us -> none  [add_band(): jnp.dot(row_data[1], onehot, precision=lax.Precision.HIGHEST)]
  transfers between devices with their start and end apart: 10 -> 0, of which waited for: 8 -> 0; matrix products, arithmetic and copies ran while one was open for 0% -> 0% of each run, Pallas kernels for 0% -> 0%
where the time goes in v1:
time: 62.9 us; the launch traced here: 62.7 us
  Pallas kernels  57 us (91%)
  local copies, waits for them, and re-layouts  5 us (8%)
  between operations  0.7 us (1%)
    pallas_call x1, Pallas kernels, shards(): pl.pallas_call(kernel, out_shape=(jax.ShapeDtypeStruct((NC, NXL, NZL, NYL...  57 us
    unnamed x18, local copies, waits for them, and re-layouts  4.11 us

profile of v1, /device:TPU:1, one launch (start us, length us, event | category | flops | bytes accessed | tf_op | source)
XLA Modules:
  0.0 62.7 jit_solution(16510072796019030258)
XLA Ops:
  0.6 0.0 copy-start.5
  0.6 0.0 copy-start.2
  0.6 1.0 %copy.11.pen_h = f32[8,12,256]{2,1,0:T(8,128)S(1)} copy(f32[8,12,256]{2,0,1:T(8,128)} %param.9) | data formatting | bytes 196608 | tf_op args[2]
  1.6 0.0 copy-done.5
  1.7 0.0 copy-done.2
  1.7 0.0 copy-start.3
  1.7 0.1 copy.9.src_h
  1.8 0.8 %copy-done.3 = f32[3,8,12,256]{3,1,2,0:T(8,128)S(1)} copy-done((f32[3,8,12,256]{3,1,2,0:T(8,128)S(1)}, f32[3,8,12,256]{3,1,2,0:T(8,128)}, u32[]{:S(2)}) %copy-start.3) | copy-done | bytes 294936
  2.7 0.0 copy-start.4
  2.7 0.1 copy.10.vel_h
  2.8 0.9 %copy-done.4 = f32[3,8,12,256]{3,1,2,0:T(8,128)S(1)} copy-done((f32[3,8,12,256]{3,1,2,0:T(8,128)S(1)}, f32[3,8,12,256]{3,1,2,0:T(8,128)}, u32[]{:S(2)}) %copy-start.4) | copy-done | bytes 294936
  3.6 0.0 copy-start
  3.6 0.0 copy-start.1
  3.6 0.1 copy.12.start_h
  3.7 0.6 copy-done
  4.3 0.0 copy-done.1
  4.3 57.0 %shard_map.86 = (f32[3,8,12,256]{3,2,1,0:T(8,128)S(1)}, f32[128]{0:T(128)S(1)}) custom-call(f32[3,8,12,256]{3,2,1,0:T(8,128)S(1)} %copy.9.src_h, f32[3,8,12,256]{3,2,1,0:T(8,128)S(1)} %copy.10.vel_h, f32[8,12,256]{2,1,0:T(8,128)S(1)} %copy.11.pen_h, f32[3,8,12,256]{3,2,1,0:T(8,128)S(1)} %copy.12.start_h, s32[8,12,256]{2,1,0:T(8,128)S(1)} %copy.13.band_h, ...), custom_call_target="tpu_custom_call" | custom-call | tf_op jit(solution)/shard_map/pallas_call | solution.py:617
  61.3 0.9 %copy.14 = f32[3,8,12,256]{3,1,2,0:T(8,128)} copy(f32[3,8,12,256]{3,2,1,0:T(8,128)S(1)} %get-tuple-element.2) | data formatting | bytes 589824 | tf_op jit(solution)/shard_map/pallas_call | solution.py:617
  62.2 0.5 copy.16
  (1 shorter events, 0.0 us)
Async XLA Ops:
  0.6 1.0 %copy-start.5 = (s32[8,12,256]{2,0,1:T(8,128)S(1)}, s32[8,12,256]{2,0,1:T(8,128)}, u32[]{:S(2)}) copy-start(s32[8,12,256]{2,0,1:T(8,128)} %param.11) | copy-start | bytes 294916
  0.6 1.1 %copy-start.2 = (f32[3,8,12,256]{3,1,2,0:T(8,128)S(1)}, f32[3,8,12,256]{3,1,2,0:T(8,128)}, u32[]{:S(2)}) copy-start(f32[3,8,12,256]{3,1,2,0:T(8,128)} %param.7) | copy-start | bytes 884740
  1.7 1.0 %copy-start.3 = (f32[3,8,12,256]{3,1,2,0:T(8,128)S(1)}, f32[3,8,12,256]{3,1,2,0:T(8,128)}, u32[]{:S(2)}) copy-start(f32[3,8,12,256]{3,1,2,0:T(8,128)} %param.8) | copy-start | bytes 884740
  2.7 1.0 %copy-start.4 = (f32[3,8,12,256]{3,1,2,0:T(8,128)S(1)}, f32[3,8,12,256]{3,1,2,0:T(8,128)}, u32[]{:S(2)}) copy-start(f32[3,8,12,256]{3,1,2,0:T(8,128)} %param.10) | copy-start | bytes 884740
  3.6 0.7 %copy-start = (s32[128]{0:T(128)S(1)}, s32[128]{0:T(128)}, u32[]{:S(2)}) copy-start(s32[128]{0:T(128)} %tb_ref.1) | copy-start | bytes 1540
  3.6 0.7 %copy-start.1 = (f32[128]{0:T(128)S(1)}, f32[128]{0:T(128)}, u32[]{:S(2)}) copy-start(f32[128]{0:T(128)} %tw_ref.1) | copy-start | bytes 1540

commit v2 on v0

v2 whole, which is shorter than its diff:
```python
import functools

import jax
import jax.numpy as jnp
from jax import lax
from jax.experimental import pallas as pl
from jax.experimental.pallas import tpu as pltpu
from jax.sharding import PartitionSpec as P

SWEEPS = 2
NBANDS = 256

STREAM = 16
CHIPS = 8
VERT = 4
SPAN = 4
NC = 3
NXL = 8
NXC = 16
NZL = 12
NYL = 256
LANES = 128

stream_coef = 1000.0
stream_conv = 200.0
cross_coef = 0.25
cross_conv = 0.25
shift_coef = 0.5

MESH = pl.DeviceIdType.MESH
F32 = jnp.float32


def kernel(
    src_h,
    vel_h,
    pen_h,
    start_h,
    band_h,
    tb_h,
    tw_h,
    out_h,
    tri_h,
    SRC,
    VEL,
    PEN,
    BAND,
    A1,
    A2,
    A3,
    PP,
    IP,
    M1,
    M2,
    M4,
    MT,
    F1,
    F2,
    F4,
    FT,
    LL,
    RC,
    YS,
    YR,
    MS,
    MR,
    CB,
    CG,
    OWN,
    S1,
    R1,
    S2,
    R2,
    AL,
    AR,
    SH,
    SL,
    OHB,
    B1S,
    B1R,
    B2S,
    B2R,
    TB,
    TW,
    TRI,
    in_sem,
    side_send,
    side_recv,
    out_sem,
    tri_sem,
    halo_send,
    halo_recv,
    m_send,
    m_recv,
    p_send,
    p_recv,
    b_send,
    b_recv,
):
    me = lax.axis_index("stream")
    mv = lax.axis_index("vert")
    mp = lax.axis_index("span")
    chip = me // 2
    q = lax.rem(me, 2)
    partner = 2 * chip + (1 - q)

    def lanes_of(half):
        return pl.ds(pl.multiple_of(half * LANES, LANES), LANES)

    def pieces(ref, dst):
        rank = len(ref.shape)
        lead = (slice(None),) * (rank - 1)
        return lambda half: ref.at[lead + (lanes_of(half),)], dst

    inner = A1.at[:, pl.ds(1, NZL)]
    inputs = (
        (start_h, inner),
        (vel_h, VEL),
        (pen_h, PEN),
        (src_h, SRC),
        (band_h, BAND),
    )

    def slot(dst, half):
        if len(dst.shape) == 5:
            return dst.at[:, :, half]
        return dst.at[:, half]

    def part(src, half):
        if len(src.shape) == 4:
            return src.at[:, :, :, lanes_of(half)]
        return src.at[:, :, lanes_of(half)]

    own_copies = []
    side_copies = []
    for i, (src, dst) in enumerate(inputs):
        own_copies.append(pltpu.make_async_copy(part(src, q), slot(dst, q), in_sem.at[i]))
        side_copies.append(
            pltpu.make_async_remote_copy(
                src_ref=part(src, 1 - q),
                dst_ref=slot(dst, q),
                send_sem=side_send.at[i],
                recv_sem=side_recv.at[i],
                device_id=(partner, mv, mp),
                device_id_type=MESH,
            )
        )
    tb_copy = pltpu.make_async_copy(tb_h, TB, tri_sem.at[0])
    tw_copy = pltpu.make_async_copy(tw_h, TW, tri_sem.at[1])

    barrier = pltpu.get_barrier_semaphore()

    def greet(j, carry):
        pl.semaphore_signal(
            barrier, inc=1, device_id=(lax.rem(me + j, STREAM), mv, mp), device_id_type=MESH
        )
        pl.semaphore_signal(
            barrier,
            inc=1,
            device_id=(me, lax.rem(mv + j // SPAN, VERT), lax.rem(mp + j % SPAN, SPAN)),
            device_id_type=MESH,
        )
        return carry

    outer_v = mv - 1 + 2 * q
    has_outer = jnp.logical_and(outer_v >= 0, outer_v < VERT)
    outer_id = (partner, lax.rem(outer_v + VERT, VERT), mp)

    nothing = jnp.zeros((2, 8, LANES), F32)
    for A in (A1, A2):
        for c in range(NC):
            A[c, 0] = nothing
            A[c, NZL + 1] = nothing
    YR[...] = jnp.zeros(YR.shape, F32)

    lax.fori_loop(1, STREAM, greet, 0)

    @pl.when(has_outer)
    def _():
        pl.semaphore_signal(barrier, inc=1, device_id=outer_id, device_id_type=MESH)

    for copy in own_copies:
        copy.start()
    tb_copy.start()
    tw_copy.start()
    pl.semaphore_wait(barrier, 2 * (STREAM - 1) + jnp.where(has_outer, 1, 0))
    for copy in side_copies:
        copy.start()

    row = lax.broadcasted_iota(jnp.int32, (8, LANES), 0)
    lane = lax.broadcasted_iota(jnp.int32, (8, LANES), 1)

    def pack_edges(k, pair, packs):
        low, high = packs
        hit = lane == k
        low = tuple(jnp.where(hit, pltpu.roll(pair[h], k, 1), low[h]) for h in range(2))
        high = tuple(jnp.where(hit, pltpu.roll(pair[h], k + 1, 1), high[h]) for h in range(2))
        return low, high

    blank = jnp.zeros((8, LANES), F32)
    no_packs = ((blank, blank), (blank, blank))

    def send_halo(s, A, packs):
        for side in range(2):
            for h in range(2):
                YS[s, side, h] = packs[side][h]

        def remote(i, src, dst, device):
            return pltpu.make_async_remote_copy(
                src_ref=src,
                dst_ref=dst,
                send_sem=halo_send.at[s, i],
                recv_sem=halo_recv.at[s, i],
                device_id=device,
                device_id_type=MESH,
            )

        copies = (
            (
                remote(0, A.at[:, NZL], A.at[:, 0], (me, mv, lax.rem(mp + 1, SPAN))),
                mp < SPAN - 1,
                mp > 0,
            ),
            (
                remote(1, A.at[:, 1], A.at[:, NZL + 1], (me, mv, lax.rem(mp + SPAN - 1, SPAN))),
                mp > 0,
                mp < SPAN - 1,
            ),
            (remote(2, YS.at[s, q], YR.at[s, 1 - q], outer_id), has_outer, has_outer),
            (remote(3, YS.at[s, 1 - q], YR.at[s, q], (partner, mv, mp)), None, None),
        )
        each(copies, 1, lambda c: c.start())
        return copies

    def each(copies, which, act):
        for item in copies:
            if item[which] is None:
                act(item[0])
            else:
                pl.when(item[which])(functools.partial(act, item[0]))

    own_copies[0].wait()
    side_copies[0].wait_recv()

    def pack_start(z, packs):
        for c in range(NC):
            packs = pack_edges(c * NZL + z, (A1[c, z + 1, 0], A1[c, z + 1, 1]), packs)
        return packs

    halo1 = send_halo(0, A1, lax.fori_loop(0, NZL, pack_start, no_packs))

    for i in (1, 2):
        own_copies[i].wait()
        side_copies[i].wait_recv()

    def flat(ref):
        count = 1
        for size in ref.shape[:-1]:
            count *= size
        return ref.reshape(count, LANES)

    velocity2, penalty2 = flat(VEL), flat(PEN)
    ip2, m2, f2 = flat(IP), flat(M1), flat(F1)
    l2, r2, p2 = flat(LL), flat(RC), flat(PP)

    def level(ref2, x, c=0):
        return ref2[pl.ds(c * NZL * NXC + x, NZL, stride=NXC), :]

    delta = jnp.ones((NZL, LANES), F32)
    for x in range(NXC):
        u = level(velocity2, x, 0)
        west = stream_coef + stream_conv * jnp.maximum(-u, 0.0)
        east = stream_coef + stream_conv * jnp.maximum(u, 0.0)
        excess = (
            (4.0 * cross_coef + shift_coef)
            + cross_conv * (jnp.abs(level(velocity2, x, 1)) + jnp.abs(level(velocity2, x, 2)))
            + level(penalty2, x)
        )
        sink = excess + west * delta
        ip = 1.0 / (east + sink)
        delta = sink * ip
        place = pl.ds(x, NZL, stride=NXC)
        ip2[place, :] = ip
        m2[place, :] = west * ip
        f2[place, :] = east * ip

    def ahead(v, n, fill):
        return jnp.where(row >= n, pltpu.roll(v, n, 0), fill)

    def behind(v, n, fill):
        return jnp.where(row < 8 - n, pltpu.roll(v, 8 - n, 0), fill)

    def fold_up(values, f1, f2, f4, ft):
        new = []
        for h in range(2):
            v = values[h]
            v = v + f1[h] * pltpu.roll(v, 7, 0)
            v = v + f2[h] * pltpu.roll(v, 6, 0)
            v = v + f4[h] * pltpu.roll(v, 4, 0)
            new.append(v)
        new[0] = new[0] + ft * jnp.broadcast_to(new[1][0:1], (8, LANES))
        return new

    def factor(z, carry):
        chains = []
        tails = []
        f1s, f2s, f4s, fts = [], [], [], []
        for h in range(2):
            m = M1[z, h]
            f = F1[z, h]
            m1 = jnp.where(row >= 1, m, 0.0)
            mm = m1 * ahead(m, 1, 0.0)
            m4 = jnp.where(row >= 4, jnp.where(row >= 2, mm, 0.0) * pltpu.roll(mm, 2, 0), 0.0)
            mm = jnp.where(row >= 2, mm, 0.0)
            M1[z, h] = m1
            M2[z, h] = mm
            M4[z, h] = m4
            t = m * ahead(m, 1, 1.0)
            t = t * ahead(t, 2, 1.0)
            chains.append(t * ahead(t, 4, 1.0))
            f1 = jnp.where(row < 7, f, 0.0)
            ff = jnp.where(row < 6, f1 * behind(f, 1, 0.0), 0.0)
            f4 = jnp.where(row < 4, ff * pltpu.roll(ff, 6, 0), 0.0)
            F1[z, h] = f1
            F2[z, h] = ff
            F4[z, h] = f4
            f1s.append(f1)
            f2s.append(ff)
            f4s.append(f4)
            t = f * behind(f, 1, 1.0)
            t = t * behind(t, 2, 1.0)
            tails.append(t * behind(t, 4, 1.0))
        MT[z] = chains[1]
        FT[z] = tails[0]
        left = [chains[0], chains[1] * jnp.broadcast_to(chains[0][7:8], (8, LANES))]
        left = fold_up(left, f1s, f2s, f4s, tails[0])
        right = [tails[0] * jnp.broadcast_to(tails[1][0:1], (8, LANES)), tails[1]]
        for h in range(2):
            LL[z, h] = left[h]
            RC[z, h] = right[h]
        return carry

    lax.fori_loop(0, NZL, factor, 0)
    for k, ref2 in enumerate((l2, r2)):
        MS[2 * k] = level(ref2, 0)
        MS[2 * k + 1] = level(ref2, NXC - 1)

    def to_chips(src_of, dst, send_sem, recv_sem):
        def send(j, carry):
            target = lax.rem(chip + j, CHIPS)
            pltpu.make_async_remote_copy(
                src_ref=src_of(target),
                dst_ref=dst.at[chip],
                send_sem=send_sem,
                recv_sem=recv_sem,
                device_id=(2 * target + q, mv, mp),
                device_id_type=MESH,
            ).start()
            return carry

        lax.fori_loop(1, CHIPS, send, 0)

    def arrive(slots, sem):
        got = slots.at[pl.ds(1, CHIPS - 1)]
        pltpu.make_async_copy(got, got, sem).wait()

    to_chips(lambda target: MS, MR, m_send, m_recv)

    for i in (3,):
        own_copies[i].wait()
        side_copies[i].wait_recv()

    first = lane == 0
    last = lane == LANES - 1

    def eliminate(s, A, halo):
        each(halo, 2, lambda c: c.wait_recv())
        edges = [[YR[s, side, h] for h in range(2)] for side in range(2)]

        def plane(z, carry):
            cross = []
            for h in range(2):
                v = VEL[1, z, h]
                w = VEL[2, z, h]
                cross.append(
                    (
                        cross_coef + cross_conv * jnp.maximum(-v, 0.0),
                        cross_coef + cross_conv * jnp.maximum(v, 0.0),
                        cross_coef + cross_conv * jnp.maximum(-w, 0.0),
                        cross_coef + cross_conv * jnp.maximum(w, 0.0),
                    )
                )
            ip = [IP[z, h] for h in range(2)]
            m1 = [M1[z, h] for h in range(2)]
            m2 = [M2[z, h] for h in range(2)]
            m4 = [M4[z, h] for h in range(2)]
            f1 = [F1[z, h] for h in range(2)]
            f2 = [F2[z, h] for h in range(2)]
            f4 = [F4[z, h] for h in range(2)]
            mt = MT[z]
            ft = FT[z]
            for c in range(NC):
                k = c * NZL + z
                o = []
                for h in range(2):
                    south, north, below, above = cross[h]
                    a = A[c, z + 1, h]
                    lo = pltpu.roll(edges[0][h], lax.rem(LANES - k, LANES), 1)
                    hi = pltpu.roll(edges[1][h], LANES - 1 - k, 1)
                    y_lo = jnp.where(first, lo, pltpu.roll(a, 1, 1))
                    y_hi = jnp.where(last, hi, pltpu.roll(a, LANES - 1, 1))
                    rhs = SRC[c, z, h] + shift_coef * a
                    rhs = rhs + south * y_lo + north * y_hi
                    rhs = rhs + below * A[c, z, h] + above * A[c, z + 2, h]
                    v = rhs * ip[h]
                    v = v + m1[h] * pltpu.roll(v, 1, 0)
                    v = v + m2[h] * pltpu.roll(v, 2, 0)
                    v = v + m4[h] * pltpu.roll(v, 4, 0)
                    o.append(v)
                o[1] = o[1] + mt * jnp.broadcast_to(o[0][7:8], (8, LANES))
                p = fold_up(o, f1, f2, f4, ft)
                for h in range(2):
                    PP[c, z, h] = p[h]
            return carry

        lax.fori_loop(0, NZL, plane, 0)

    eliminate(0, A1, halo1)
    for c in range(NC):
        S1[0, c] = level(p2, 0, c)
        S1[1, c] = level(p2, NXC - 1, c)
    to_chips(lambda target: S1, R1, p_send.at[0], p_recv.at[0])

    own_copies[4].wait()
    side_copies[4].wait_recv()
    iota16 = lax.broadcasted_iota(jnp.int32, (16, LANES), 0)

    def onehot(z, carry):
        for h in range(2):
            low_part = lax.rem(BAND[z, h], 16)
            for i in range(8):
                at = (8 * h + i) * LANES
                OHB[z, :, at : at + LANES] = jnp.where(
                    jnp.broadcast_to(low_part[i : i + 1], (16, LANES)) == iota16, 1.0, 0.0
                ).astype(jnp.bfloat16)
        return carry

    lax.fori_loop(0, NZL, onehot, 0)

    arrive(MR, m_recv)

    def upstream(k, F):
        lf, lg, rf, rg = (MR[k, i] for i in range(4))
        b = lg / (1.0 - lf * F)
        g = b * F
        CB[k] = b
        CG[k] = g
        return rg + g * rf

    def downstream(i, H):
        k = CHIPS - 1 - i
        lf, lg, rf, rg = (MR[k, i] for i in range(4))
        b = rf / (1.0 - rg * H)
        g = b * H
        CB[k] = b
        CG[k] = g
        return lf + g * lg

    none = jnp.zeros((NZL, LANES), F32)
    F = lax.fori_loop(0, chip, upstream, none)
    H = lax.fori_loop(0, CHIPS - 1 - chip, downstream, none)
    lf, lg, rf, rg = (MS[i] for i in range(4))
    from_left = 1.0 - lf * F
    from_right = 1.0 - rg * H
    inv = 1.0 / (from_left * from_right - (F * rf) * (H * lg))
    for i, value in enumerate(
        (
            F,
            H,
            from_right * inv,
            F * rf * inv,
            H * lg * inv,
            from_left * inv,
            lg / from_left * F,
            rf / from_right * H,
        )
    ):
        OWN[i] = value

    def close(incoming):
        for c in range(NC):
            first_p = level(p2, 0, c)
            last_p = level(p2, NXC - 1, c)
            x = OWN[0] * first_p + incoming[0][c]
            y = OWN[1] * last_p + incoming[1][c]
            AL[c] = OWN[2] * x + OWN[3] * y
            AR[c] = OWN[4] * x + OWN[5] * y

    def solved(c, z, h):
        return (
            PP[c, z, h]
            + LL[z, h] * jnp.broadcast_to(AL[c, pl.ds(z, 1), :], (8, LANES))
            + RC[z, h] * jnp.broadcast_to(AR[c, pl.ds(z, 1), :], (8, LANES))
        )

    arrive(R1, p_recv.at[0])
    trio = (none,) * NC

    def up_first(k, O):
        return tuple(R1[k, 1, c] + CG[k] * R1[k, 0, c] + CB[k] * O[c] for c in range(NC))

    def down_first(i, Q):
        k = CHIPS - 1 - i
        return tuple(R1[k, 0, c] + CG[k] * R1[k, 1, c] + CB[k] * Q[c] for c in range(NC))

    close(
        (
            lax.fori_loop(0, chip, up_first, trio),
            lax.fori_loop(0, CHIPS - 1 - chip, down_first, trio),
        )
    )

    def line_first(z, packs):
        for c in range(NC):
            pair = tuple(solved(c, z, h) for h in range(2))
            for h in range(2):
                A2[c, z + 1, h] = pair[h]
            packs = pack_edges(c * NZL + z, pair, packs)
        return packs

    halo2 = send_halo(1, A2, lax.fori_loop(0, NZL, line_first, no_packs))

    eliminate(1, A2, halo2)
    for c in range(NC):
        first_p = level(p2, 0, c)
        last_p = level(p2, NXC - 1, c)
        S2[0, c] = last_p + OWN[6] * first_p
        S2[1, c] = first_p + OWN[7] * last_p
    to_chips(
        lambda target: S2.at[jnp.where(target > chip, 0, 1)], R2, p_send.at[1], p_recv.at[1]
    )
    arrive(R2, p_recv.at[1])

    def up_second(k, O):
        return tuple(R2[k, c] + CB[k] * O[c] for c in range(NC))

    def down_second(i, Q):
        k = CHIPS - 1 - i
        return tuple(R2[k, c] + CB[k] * Q[c] for c in range(NC))

    close(
        (
            lax.fori_loop(0, chip, up_second, trio),
            lax.fori_loop(0, CHIPS - 1 - chip, down_second, trio),
        )
    )

    def line_last(z, carry):
        for h in range(2):
            total = None
            for c in range(NC):
                a = solved(c, z, h)
                A3[c, z, h] = a
                term = VEL[c, z, h] * a
                total = term if total is None else total + term
            total = total * PEN[z, h]
            coarse = total.astype(jnp.bfloat16).astype(F32)
            SH[z, h] = coarse
            SL[z, h] = total - coarse
        return carry

    lax.fori_loop(0, NZL, line_last, 0)
    out_own = pltpu.make_async_copy(A3.at[:, :, q], out_h.at[:, :, :, lanes_of(q)], out_sem.at[0])
    out_side = pltpu.make_async_remote_copy(
        src_ref=A3.at[:, :, 1 - q],
        dst_ref=out_h.at[:, :, :, lanes_of(q)],
        send_sem=out_sem.at[1],
        recv_sem=out_sem.at[2],
        device_id=(partner, mv, mp),
        device_id_type=MESH,
    )
    out_own.start()
    out_side.start()

    def band_rows(z, acc):
        parts = []
        for h in range(2):
            high_part = BAND[z, h] // 16
            coarse = SH[z, h]
            fine = SL[z, h]
            for i in range(8):
                hit = jnp.broadcast_to(high_part[i : i + 1], (16, LANES)) == iota16
                parts.append(
                    jnp.concatenate(
                        [
                            jnp.where(hit, jnp.broadcast_to(v[i : i + 1], (16, LANES)), 0.0)
                            for v in (coarse, fine)
                        ],
                        axis=0,
                    ).astype(jnp.bfloat16)
                )
        weights = jnp.concatenate(parts, axis=1)
        return acc + lax.dot_general(
            weights, OHB[z], (((1,), (1,)), ((), ())), preferred_element_type=F32
        )

    acc = lax.fori_loop(0, NZL, band_rows, jnp.zeros((32, 16), F32))
    sums = acc[0:16] + acc[16:32]
    wide = jnp.concatenate([sums] * 8, axis=1)
    keep = lane // 16 == row
    for h in range(2):
        B1S[h : h + 1, :] = jnp.sum(
            jnp.where(keep, wide[8 * h : 8 * h + 8], 0.0), axis=0, keepdims=True
        )

    def band_round(r, own, slots, device_of):
        def send(j, carry):
            pltpu.make_async_remote_copy(
                src_ref=own,
                dst_ref=slots.at[j],
                send_sem=b_send.at[r],
                recv_sem=b_recv.at[r],
                device_id=device_of(j),
                device_id_type=MESH,
            ).start()
            return carry

        lax.fori_loop(1, STREAM, send, 0)
        got = slots.at[pl.ds(1, STREAM - 1)]
        pltpu.make_async_copy(got, got, b_recv.at[r]).wait()
        total = own[...]
        for j in range(1, STREAM):
            total = total + slots[j]
        return total

    B2S[...] = band_round(0, B1S, B1R, lambda j: (lax.rem(me + j, STREAM), mv, mp))
    bands = band_round(
        1,
        B2S,
        B2R,
        lambda j: (me, lax.rem(mv + j // SPAN, VERT), lax.rem(mp + j % SPAN, SPAN)),
    )
    cells = STREAM * VERT * SPAN * NXL * NZL * NYL
    bands = bands * ((NBANDS / cells) ** 0.5)
    tb_copy.wait()
    tw_copy.wait()
    tb = TB[...].reshape(1, LANES)
    spot = jnp.broadcast_to(lax.rem(tb, LANES), (8, LANES))
    low_half = jnp.take_along_axis(jnp.broadcast_to(bands[0:1], (8, LANES)), spot, axis=1)
    high_half = jnp.take_along_axis(jnp.broadcast_to(bands[1:2], (8, LANES)), spot, axis=1)
    picked = jnp.where(tb < LANES, low_half[0:1], high_half[0:1])
    TRI[...] = (TW[...].reshape(1, LANES) * picked).reshape(LANES)
    tri_copy = pltpu.make_async_copy(TRI, tri_h, tri_sem.at[2])
    tri_copy.start()

    def drain(count, ref, sem):
        def one(j, carry):
            pltpu.make_async_copy(ref, ref, sem).wait()
            return carry

        lax.fori_loop(0, count, one, 0)

    for copy in side_copies:
        copy.wait_send()
    each(halo1, 1, lambda c: c.wait_send())
    each(halo2, 1, lambda c: c.wait_send())
    drain(CHIPS - 1, MS, m_send)
    drain(CHIPS - 1, S1, p_send.at[0])
    drain(CHIPS - 1, S2.at[0], p_send.at[1])
    for r, own in enumerate((B1S, B2S)):
        drain(STREAM - 1, own, b_send.at[r])
    out_own.wait()
    out_side.wait()
    tri_copy.wait()


def shards(adjoint_source, velocity, penalty, adjoint_start, cell_band, tri_band, tri_weight):
    anywhere = pl.BlockSpec(memory_space=pl.ANY)

    def field():
        return pltpu.VMEM((NZL, 2, 8, LANES), F32)

    scratch = [
        pltpu.VMEM((NC, NZL, 2, 8, LANES), F32),
        pltpu.VMEM((NC, NZL, 2, 8, LANES), F32),
        field(),
        pltpu.VMEM((NZL, 2, 8, LANES), jnp.int32),
        pltpu.VMEM((NC, NZL + 2, 2, 8, LANES), F32),
        pltpu.VMEM((NC, NZL + 2, 2, 8, LANES), F32),
        pltpu.VMEM((NC, NZL, 2, 8, LANES), F32),
        pltpu.VMEM((NC, NZL, 2, 8, LANES), F32),
        field(),
        field(),
        field(),
        field(),
        pltpu.VMEM((NZL, 8, LANES), F32),
        field(),
        field(),
        field(),
        pltpu.VMEM((NZL, 8, LANES), F32),
        field(),
        field(),
        pltpu.VMEM((SWEEPS, 2, 2, 8, LANES), F32),
        pltpu.VMEM((SWEEPS, 2, 2, 8, LANES), F32),
        pltpu.VMEM((4, NZL, LANES), F32),
        pltpu.VMEM((CHIPS, 4, NZL, LANES), F32),
        pltpu.VMEM((CHIPS, NZL, LANES), F32),
        pltpu.VMEM((CHIPS, NZL, LANES), F32),
        pltpu.VMEM((8, NZL, LANES), F32),
        pltpu.VMEM((2, NC, NZL, LANES), F32),
        pltpu.VMEM((CHIPS, 2, NC, NZL, LANES), F32),
        pltpu.VMEM((2, NC, NZL, LANES), F32),
        pltpu.VMEM((CHIPS, NC, NZL, LANES), F32),
        pltpu.VMEM((NC, NZL, LANES), F32),
        pltpu.VMEM((NC, NZL, LANES), F32),
        field(),
        field(),
        pltpu.VMEM((NZL, 16, NXC * LANES), jnp.bfloat16),
        pltpu.VMEM((2, LANES), F32),
        pltpu.VMEM((STREAM, 2, LANES), F32),
        pltpu.VMEM((2, LANES), F32),
        pltpu.VMEM((STREAM, 2, LANES), F32),
        pltpu.VMEM((LANES,), jnp.int32),
        pltpu.VMEM((LANES,), F32),
        pltpu.VMEM((LANES,), F32),
        pltpu.SemaphoreType.DMA((5,)),
        pltpu.SemaphoreType.DMA((5,)),
        pltpu.SemaphoreType.DMA((5,)),
        pltpu.SemaphoreType.DMA((3,)),
        pltpu.SemaphoreType.DMA((3,)),
        pltpu.SemaphoreType.DMA((SWEEPS, 4)),
        pltpu.SemaphoreType.DMA((SWEEPS, 4)),
        pltpu.SemaphoreType.DMA,
        pltpu.SemaphoreType.DMA,
        pltpu.SemaphoreType.DMA((SWEEPS,)),
        pltpu.SemaphoreType.DMA((SWEEPS,)),
        pltpu.SemaphoreType.DMA((2,)),
        pltpu.SemaphoreType.DMA((2,)),
    ]

    def planes(x):
        return jnp.swapaxes(x, -3, -2)

    adjoint, tri_grad = pl.pallas_call(
        kernel,
        out_shape=(
            jax.ShapeDtypeStruct((NC, NZL, NXL, NYL), F32),
            jax.ShapeDtypeStruct((LANES,), F32),
        ),
        in_specs=[anywhere] * 7,
        out_specs=(anywhere, anywhere),
        scratch_shapes=scratch,
        compiler_params=pltpu.CompilerParams(
            collective_id=0, has_side_effects=True, vmem_limit_bytes=56 * 1024 * 1024
        ),
    )(
        planes(adjoint_source),
        planes(velocity),
        planes(penalty),
        planes(adjoint_start),
        planes(cell_band),
        tri_band,
        tri_weight,
    )
    return planes(adjoint), tri_grad


def solution(mesh):
    return jax.shard_map(
        shards,
        mesh=mesh,
        in_specs=(
            P(None, "stream", "span", "vert"),
            P(None, "stream", "span", "vert"),
            P("stream", "span", "vert"),
            P(None, "stream", "span", "vert"),
            P("stream", "span", "vert"),
            P(("stream", "vert", "span")),
            P(("stream", "vert", "span")),
        ),
        out_specs=(P(None, "stream", "span", "vert"), P(("stream", "vert", "span"))),
        check_vma=False,
    )
```

time: 403 us -> 54.2 us (0.13)
  blocking collectives: 146 us -> 0 us
  waiting for transfers between devices: 125 us -> 0 us
  local copies, waits for them, and re-layouts: 64.9 us -> 2.21 us
  Pallas kernels: 0 us -> 51.2 us
  starting transfers between devices: 18.6 us -> 0 us
  other arithmetic: 17.6 us -> 0 us
  between operations: 14.6 us -> 0.65 us
  matrix products: 8.88 us -> 0 us
  loops' own time: 4.2 us -> 0 us
    all_gather x2 -> x0, waiting for transfers between devices: 107 us -> none  [prefix_2(): everything = jax.tree.map(lambda part: lax.all_gather(part, axis), x)]
    psum x1 -> x0, blocking collectives: 76.4 us -> none  [shards(): band_sums = lax.psum(partial_sums, ('stream', 'vert', 'span')) * band_scale]
    all_gather x4 -> x0, blocking collectives: 69.5 us -> none  [prefix_2(): everything = jax.tree.map(lambda part: lax.all_gather(part, axis), x)]
    pallas_call x0 -> x1, Pallas kernels: none -> 51.2 us  [shards(): pl.pallas_call(kernel, out_shape=(jax.ShapeDtypeStruct((NC, NZL, NXL, NYL...]
    mul x80 -> x0, local copies, waits for them, and re-layouts: 45.5 us -> none  [the longest x32 33.5 us: multiply(): return jnp.sum(left_mat[:, :, None] * right_mat[None, :, :], axis=1)]
    ppermute x8 -> x0, starting transfers between devices: 18.5 us -> none  [the longest x4 13.4 us: padded_2(): lax.ppermute(lax.slice_in_dim(block, block.shape[dim] - width, None, axis...]
    ppermute x8 -> x0, waiting for transfers between devices: 17.9 us -> none  [the longest x4 14.4 us: padded_2(): lax.ppermute(lax.slice_in_dim(block, 0, width, axis=dim), axis, backward)]
    dot_general x8 -> x0, matrix products: 8.88 us -> none  [add_band(): jnp.dot(row_data[1], onehot, precision=lax.Precision.HIGHEST)]
  transfers between devices with their start and end apart: 10 -> 0, of which waited for: 8 -> 0; matrix products, arithmetic and copies ran while one was open for 0% -> 0% of each run, Pallas kernels for 0% -> 0%
where the time goes in v2:
time: 54.2 us; the launch traced here: 54.1 us
  Pallas kernels  51.2 us (94%)
  local copies, waits for them, and re-layouts  2.21 us (4%)
  between operations  0.65 us (1%)
    pallas_call x1, Pallas kernels, shards(): pl.pallas_call(kernel, out_shape=(jax.ShapeDtypeStruct((NC, NZL, NXL, NYL...  51.2 us
    unnamed x4, local copies, waits for them, and re-layouts  2.21 us

profile of v2, /device:TPU:1, one launch (start us, length us, event | category | flops | bytes accessed | tf_op | source)
XLA Modules:
  0.0 54.1 jit_solution(16267535611266565648)
XLA Ops:
  0.6 51.2 %shard_map.86 = (f32[3,12,8,256]{3,2,1,0:T(8,128)}, f32[128]{0:T(128)}) custom-call(f32[3,12,8,256]{3,2,1,0:T(8,128)} %bitcast.6, f32[3,12,8,256]{3,2,1,0:T(8,128)} %bitcast.7, f32[12,8,256]{2,1,0:T(8,128)} %bitcast.10, f32[3,12,8,256]{3,2,1,0:T(8,128)} %bitcast.8, s32[12,8,256]{2,1,0:T(8,128)} %bitcast.11, s32[128]{0:T(128)} %tb_h.1, f32[128]{0:T(128)} %tw_h.1), custom_call_target="tpu_custom_call" | custom-call | tf_op jit(solution)/shard_map/pallas_call | solution.py:744
  51.9 0.0 copy-start
  51.9 1.7 %copy.11 = f32[3,8,12,256]{3,1,2,0:T(8,128)} copy(f32[3,8,12,256]{3,1,2,0:T(8,128)} %bitcast.9) | data formatting | bytes 589824
  53.6 0.0 copy-done
  53.6 0.5 copy.12
Async XLA Ops:
  51.9 1.7 %copy-start = (f32[128]{0:T(128)S(1)}, f32[128]{0:T(128)}, u32[]{:S(2)}) copy-start(f32[128]{0:T(128)} %get-tuple-element.9) | copy-start | bytes 1540

commit v3 on v2

--- a/solution.py
+++ b/solution.py
@@ -20,6 +20,7 @@
 NZL = 12
 NYL = 256
 LANES = 128
+OWNERS = 6
 
 stream_coef = 1000.0
 stream_conv = 200.0
@@ -60,6 +61,8 @@
     FT,
     LL,
     RC,
+    STG,
+    YF,
     YS,
     YR,
     MS,
@@ -67,7 +70,13 @@
     CB,
     CG,
     OWN,
+    QS,
+    QR,
+    CO,
+    OC,
     S1,
+    G1,
+    D1,
     R1,
     S2,
     R2,
@@ -88,10 +97,20 @@
     side_recv,
     out_sem,
     tri_sem,
+    LT,
+    LP,
+    fz_send,
+    fz_recv,
+    fv_send,
+    fv_recv,
     halo_send,
     halo_recv,
     m_send,
     m_recv,
+    q_send,
+    q_recv,
+    d_send,
+    d_recv,
     p_send,
     p_recv,
     b_send,
@@ -150,17 +169,26 @@
 
     barrier = pltpu.get_barrier_semaphore()
 
-    def greet(j, carry):
-        pl.semaphore_signal(
-            barrier, inc=1, device_id=(lax.rem(me + j, STREAM), mv, mp), device_id_type=MESH
-        )
-        pl.semaphore_signal(
-            barrier,
-            inc=1,
-            device_id=(me, lax.rem(mv + j // SPAN, VERT), lax.rem(mp + j % SPAN, SPAN)),
-            device_id_type=MESH,
-        )
-        return carry
+    def either(condition):
+        return jnp.where(condition, 1, 0)
+
+    has_v = (mv > 0, mv < VERT - 1)
+    has_p = (mp > 0, mp < SPAN - 1)
+    v_near = either(has_v[0]) + either(has_v[1])
+    p_near = either(has_p[0]) + either(has_p[1])
+
+    def call(sem, device):
+        pl.semaphore_signal(sem, inc=1, device_id=device, device_id_type=MESH)
+
+    def stream_at(step):
+        return (lax.rem(me + 2 * step + STREAM, STREAM), mv, mp)
+
+    def call_line(sem, along_v):
+        for i, step in enumerate((-1, 1)):
+            if along_v:
+                pl.when(has_v[i])(lambda: call(sem, (me, mv + step, mp)))
+            else:
+                pl.when(has_p[i])(lambda: call(sem, (me, mv, mp + step)))
 
     outer_v = mv - 1 + 2 * q
     has_outer = jnp.logical_and(outer_v >= 0, outer_v < VERT)
@@ -173,19 +201,27 @@
             A[c, NZL + 1] = nothing
     YR[...] = jnp.zeros(YR.shape, F32)
 
-    lax.fori_loop(1, STREAM, greet, 0)
-
-    @pl.when(has_outer)
-    def _():
-        pl.semaphore_signal(barrier, inc=1, device_id=outer_id, device_id_type=MESH)
-
-    for copy in own_copies:
-        copy.start()
+    call(barrier, (partner, mv, mp))
+    call(barrier, stream_at(-1))
+    call(barrier, stream_at(1))
+    for i, step in enumerate((-1, 1)):
+        for core in range(2):
+            other = 2 * chip + core
+            pl.when(has_v[i])(lambda: call(barrier, (other, mv + step, mp)))
+            pl.when(has_p[i])(lambda: call(barrier, (other, mv, mp + step)))
+
+    stage = pltpu.make_async_copy(start_h, STG, in_sem.at[5])
+    stage.start()
+    for i in (1, 2, 0, 3, 4):
+        own_copies[i].start()
     tb_copy.start()
     tw_copy.start()
-    pl.semaphore_wait(barrier, 2 * (STREAM - 1) + jnp.where(has_outer, 1, 0))
-    for copy in side_copies:
-        copy.start()
+    pl.semaphore_wait(barrier, 3 + 2 * v_near + 2 * p_near)
+    for i in range(3):
+        side_copies[i].start()
+    call(LT.at[0], stream_at(-1))
+    call(LT.at[0], stream_at(1))
+    call_line(LP.at[0], True)
 
     row = lax.broadcasted_iota(jnp.int32, (8, LANES), 0)
     lane = lax.broadcasted_iota(jnp.int32, (8, LANES), 1)
@@ -239,15 +275,74 @@
             else:
                 pl.when(item[which])(functools.partial(act, item[0]))
 
-    own_copies[0].wait()
-    side_copies[0].wait_recv()
+    first_halo = []
+    for i, step in enumerate((-1, 1)):
+        for core in range(2):
+            first_halo.append(
+                (
+                    pltpu.make_async_remote_copy(
+                        src_ref=start_h.at[:, (0, NZL - 1)[i], :, pl.ds(core * LANES, LANES)],
+                        dst_ref=A1.at[:, (NZL + 1, 0)[i], q],
+                        send_sem=fz_send.at[i, core],
+                        recv_sem=fz_recv.at[i, q],
+                        device_id=(2 * chip + core, mv, mp + step),
+                        device_id_type=MESH,
+                    ),
+                    has_p[i],
+                )
+            )
+    for copy, there in first_halo:
+        pl.when(there)(copy.start)
+
+    stage.wait()
 
     def pack_start(z, packs):
+        low, high = packs
         for c in range(NC):
-            packs = pack_edges(c * NZL + z, (A1[c, z + 1, 0], A1[c, z + 1, 1]), packs)
-        return packs
-
-    halo1 = send_halo(0, A1, lax.fori_loop(0, NZL, pack_start, no_packs))
+            pair = (STG[c, z, :, 0:LANES], STG[c, z, :, LANES:NYL])
+            low, high = pack_edges(c * NZL + z, pair, (low, high))
+        return low, high
+
+    low, high = lax.fori_loop(0, NZL, pack_start, no_packs)
+    for i, value in enumerate((low[0], high[1], high[0], low[1])):
+        YF[i] = value
+    for i, step in enumerate((-1, 1)):
+        copy = pltpu.make_async_remote_copy(
+            src_ref=YF.at[i],
+            dst_ref=YR.at[0, 1 - i, q],
+            send_sem=fv_send.at[i],
+            recv_sem=fv_recv.at[q],
+            device_id=(2 * chip + 1 - i, mv + step, mp),
+            device_id_type=MESH,
+        )
+        first_halo.append((copy, has_v[i]))
+        pl.when(has_v[i])(copy.start)
+    middle = pltpu.make_async_remote_copy(
+        src_ref=YF.at[2 + q],
+        dst_ref=YR.at[0, q, q],
+        send_sem=fv_send.at[2],
+        recv_sem=fv_recv.at[2],
+        device_id=(partner, mv, mp),
+        device_id_type=MESH,
+    )
+    middle.start()
+    YR[0, 1 - q, q] = YF[3 - q]
+
+    def first_arrivals():
+        for i in range(2):
+            for sender in range(2):
+                slab = A1.at[:, (0, NZL + 1)[i], sender]
+                pl.when(has_p[i])(
+                    lambda: pltpu.make_async_copy(slab, slab, fz_recv.at[1 - i, sender]).wait()
+                )
+        for sender in range(2):
+            pl.when(has_outer)(
+                lambda: pltpu.make_async_copy(YF.at[0], YF.at[0], fv_recv.at[sender]).wait()
+            )
+        middle.wait_recv()
+
+    for i in range(3, 5):
+        side_copies[i].start()
 
     for i in (1, 2):
         own_copies[i].wait()
@@ -364,7 +459,44 @@
         got = slots.at[pl.ds(1, CHIPS - 1)]
         pltpu.make_async_copy(got, got, sem).wait()
 
-    to_chips(lambda target: MS, MR, m_send, m_recv)
+    pl.semaphore_wait(LT.at[0], 2)
+    call(LT.at[1], stream_at(-2))
+    call(LT.at[1], stream_at(2))
+    pl.semaphore_wait(LT.at[1], 2)
+    call(LT.at[2], (partner, mv, mp))
+
+    is_owner = lax.rem(chip, 4) < 3
+    my_o = (chip // 4) * 3 + lax.rem(chip, 4)
+    owner_sends = jnp.where(is_owner, OWNERS - 1, OWNERS)
+
+    def to_owners(src_of, dst, send_sem, recv_sem):
+        def send(o, carry):
+            target = o + o // 3
+
+            @pl.when(target != chip)
+            def _():
+                pltpu.make_async_remote_copy(
+                    src_ref=src_of(o),
+                    dst_ref=dst,
+                    send_sem=send_sem,
+                    recv_sem=recv_sem,
+                    device_id=(2 * target + q, mv, mp),
+                    device_id_type=MESH,
+                ).start()
+
+            @pl.when(target == chip)
+            def _():
+                pltpu.make_async_copy(src_of(o), dst, recv_sem).start()
+
+            return carry
+
+        lax.fori_loop(0, OWNERS, send, 0)
+
+    for k in range(4):
+        value = MS[k]
+        for o in range(OWNERS):
+            QS[k, o] = value[2 * o : 2 * o + 2]
+    to_owners(lambda o: QS.at[:, o], QR.at[chip], q_send, q_recv)
 
     for i in (3,):
         own_copies[i].wait()
@@ -373,8 +505,7 @@
     first = lane == 0
     last = lane == LANES - 1
 
-    def eliminate(s, A, halo):
-        each(halo, 2, lambda c: c.wait_recv())
+    def eliminate(s, A):
         edges = [[YR[s, side, h] for h in range(2)] for side in range(2)]
 
         def plane(z, carry):
@@ -425,11 +556,21 @@
 
         lax.fori_loop(0, NZL, plane, 0)
 
-    eliminate(0, A1, halo1)
+    own_copies[0].wait()
+    side_copies[0].wait_recv()
+    first_arrivals()
+    pl.semaphore_wait(LP.at[0], v_near)
+    call_line(LP.at[1], True)
+    eliminate(0, A1)
     for c in range(NC):
-        S1[0, c] = level(p2, 0, c)
-        S1[1, c] = level(p2, NXC - 1, c)
-    to_chips(lambda target: S1, R1, p_send.at[0], p_recv.at[0])
+        for i, x in enumerate((0, NXC - 1)):
+            value = level(p2, x, c)
+            for o in range(OWNERS):
+                S1[i, c, o] = value[2 * o : 2 * o + 2]
+    to_owners(lambda o: S1.at[:, :, o], G1.at[chip], p_send.at[0], p_recv.at[0])
+    pl.semaphore_wait(LP.at[1], v_near)
+    call_line(LP.at[2], False)
+    to_chips(lambda target: MS, MR, m_send, m_recv)
 
     own_copies[4].wait()
     side_copies[4].wait_recv()
@@ -446,6 +587,49 @@
         return carry
 
     lax.fori_loop(0, NZL, onehot, 0)
+
+    @pl.when(is_owner)
+    def _():
+        pltpu.make_async_copy(QR, QR, q_recv).wait()
+        ahead_f = jnp.zeros((2, LANES), F32)
+        for k in range(CHIPS):
+            lf, lg, rf, rg = (QR[k, i] for i in range(4))
+            inv = 1.0 / (1.0 - lf * ahead_f)
+            b = lg * inv
+            g = b * ahead_f
+            for i, value in enumerate((g, b, inv, lf * inv, rf * inv, ahead_f)):
+                CO[k, i] = value
+            ahead_f = rg + g * rf
+
+        pltpu.make_async_copy(G1, G1, p_recv.at[0]).wait()
+        nil = jnp.zeros((2, LANES), F32)
+        O = [nil] * NC
+        for k in range(CHIPS):
+            for c in range(NC):
+                OC[k, c] = O[c]
+                O[c] = G1[k, 1, c] + CO[k, 0] * G1[k, 0, c] + CO[k, 1] * O[c]
+        after = [nil] * NC
+        for k in reversed(range(CHIPS)):
+            for c in range(NC):
+                D1[k, 1, c] = after[c]
+                before = OC[k, c]
+                after[c] = CO[k, 2] * G1[k, 0, c] + CO[k, 3] * before + CO[k, 4] * after[c]
+                D1[k, 0, c] = CO[k, 5] * after[c] + before
+
+        def reply(j, carry):
+            target = lax.rem(chip + j, CHIPS)
+            pltpu.make_async_remote_copy(
+                src_ref=D1.at[target],
+                dst_ref=R1.at[:, :, my_o],
+                send_sem=d_send,
+                recv_sem=d_recv,
+                device_id=(2 * target + q, mv, mp),
+                device_id_type=MESH,
+            ).start()
+            return carry
+
+        lax.fori_loop(1, CHIPS, reply, 0)
+        pltpu.make_async_copy(D1.at[chip], R1.at[:, :, my_o], d_recv).start()
 
     arrive(MR, m_recv)
 
@@ -503,22 +687,14 @@
             + RC[z, h] * jnp.broadcast_to(AR[c, pl.ds(z, 1), :], (8, LANES))
         )
 
-    arrive(R1, p_recv.at[0])
+    pltpu.make_async_copy(R1, R1, d_recv).wait()
+    pl.semaphore_wait(LP.at[2], p_near)
+    call_line(LP.at[3], False)
     trio = (none,) * NC
-
-    def up_first(k, O):
-        return tuple(R1[k, 1, c] + CG[k] * R1[k, 0, c] + CB[k] * O[c] for c in range(NC))
-
-    def down_first(i, Q):
-        k = CHIPS - 1 - i
-        return tuple(R1[k, 0, c] + CG[k] * R1[k, 1, c] + CB[k] * Q[c] for c in range(NC))
-
-    close(
-        (
-            lax.fori_loop(0, chip, up_first, trio),
-            lax.fori_loop(0, CHIPS - 1 - chip, down_first, trio),
-        )
-    )
+    for c in range(NC):
+        for o in range(OWNERS):
+            AL[c, 2 * o : 2 * o + 2, :] = R1[0, c, o]
+            AR[c, 2 * o : 2 * o + 2, :] = R1[1, c, o]
 
     def line_first(z, packs):
         for c in range(NC):
@@ -530,7 +706,10 @@
 
     halo2 = send_halo(1, A2, lax.fori_loop(0, NZL, line_first, no_packs))
 
-    eliminate(1, A2, halo2)
+    each(halo2, 2, lambda c: c.wait_recv())
+    pl.semaphore_wait(LP.at[3], p_near)
+    call_line(LP.at[4], False)
+    eliminate(1, A2)
     for c in range(NC):
         first_p = level(p2, 0, c)
         last_p = level(p2, NXC - 1, c)
@@ -570,18 +749,6 @@
         return carry
 
     lax.fori_loop(0, NZL, line_last, 0)
-    out_own = pltpu.make_async_copy(A3.at[:, :, q], out_h.at[:, :, :, lanes_of(q)], out_sem.at[0])
-    out_side = pltpu.make_async_remote_copy(
-        src_ref=A3.at[:, :, 1 - q],
-        dst_ref=out_h.at[:, :, :, lanes_of(q)],
-        send_sem=out_sem.at[1],
-        recv_sem=out_sem.at[2],
-        device_id=(partner, mv, mp),
-        device_id_type=MESH,
-    )
-    out_own.start()
-    out_side.start()
-
     def band_rows(z, acc):
         parts = []
         for h in range(2):
@@ -604,6 +771,8 @@
             weights, OHB[z], (((1,), (1,)), ((), ())), preferred_element_type=F32
         )
 
+    pl.semaphore_wait(LT.at[2], 1)
+    pl.semaphore_wait(LP.at[4], p_near)
     acc = lax.fori_loop(0, NZL, band_rows, jnp.zeros((32, 16), F32))
     sums = acc[0:16] + acc[16:32]
     wide = jnp.concatenate([sums] * 8, axis=1)
@@ -613,7 +782,7 @@
             jnp.where(keep, wide[8 * h : 8 * h + 8], 0.0), axis=0, keepdims=True
         )
 
-    def band_round(r, own, slots, device_of):
+    def band_round(r, own, slots, device_of, beside):
         def send(j, carry):
             pltpu.make_async_remote_copy(
                 src_ref=own,
@@ -626,6 +795,7 @@
             return carry
 
         lax.fori_loop(1, STREAM, send, 0)
+        beside()
         got = slots.at[pl.ds(1, STREAM - 1)]
         pltpu.make_async_copy(got, got, b_recv.at[r]).wait()
         total = own[...]
@@ -633,12 +803,27 @@
             total = total + slots[j]
         return total
 
-    B2S[...] = band_round(0, B1S, B1R, lambda j: (lax.rem(me + j, STREAM), mv, mp))
+    out_own = pltpu.make_async_copy(A3.at[:, :, q], out_h.at[:, :, :, lanes_of(q)], out_sem.at[0])
+    out_side = pltpu.make_async_remote_copy(
+        src_ref=A3.at[:, :, 1 - q],
+        dst_ref=out_h.at[:, :, :, lanes_of(q)],
+        send_sem=out_sem.at[1],
+        recv_sem=out_sem.at[2],
+        device_id=(partner, mv, mp),
+        device_id_type=MESH,
+    )
+
+    def send_out():
+        out_own.start()
+        out_side.start()
+
+    B2S[...] = band_round(0, B1S, B1R, lambda j: (lax.rem(me + j, STREAM), mv, mp), send_out)
     bands = band_round(
         1,
         B2S,
         B2R,
         lambda j: (me, lax.rem(mv + j // SPAN, VERT), lax.rem(mp + j % SPAN, SPAN)),
+        lambda: None,
     )
     cells = STREAM * VERT * SPAN * NXL * NZL * NYL
     bands = bands * ((NBANDS / cells) ** 0.5)
@@ -662,10 +847,18 @@
 
     for copy in side_copies:
         copy.wait_send()
-    each(halo1, 1, lambda c: c.wait_send())
+    for copy, there in first_halo:
+        pl.when(there)(copy.wait_send)
+    middle.wait_send()
     each(halo2, 1, lambda c: c.wait_send())
     drain(CHIPS - 1, MS, m_send)
-    drain(CHIPS - 1, S1, p_send.at[0])
+    drain(owner_sends, QS.at[:, 0], q_send)
+    drain(owner_sends, S1.at[:, :, 0], p_send.at[0])
+
+    @pl.when(is_owner)
+    def _():
+        drain(CHIPS - 1, D1.at[0], d_send)
+
     drain(CHIPS - 1, S2.at[0], p_send.at[1])
     for r, own in enumerate((B1S, B2S)):
         drain(STREAM - 1, own, b_send.at[r])
@@ -700,6 +893,8 @@
         pltpu.VMEM((NZL, 8, LANES), F32),
         field(),
         field(),
+        pltpu.VMEM((NC, NZL, NXL, NYL), F32),
+        pltpu.VMEM((4, 8, LANES), F32),
         pltpu.VMEM((SWEEPS, 2, 2, 8, LANES), F32),
         pltpu.VMEM((SWEEPS, 2, 2, 8, LANES), F32),
         pltpu.VMEM((4, NZL, LANES), F32),
@@ -707,8 +902,14 @@
         pltpu.VMEM((CHIPS, NZL, LANES), F32),
         pltpu.VMEM((CHIPS, NZL, LANES), F32),
         pltpu.VMEM((8, NZL, LANES), F32),
-        pltpu.VMEM((2, NC, NZL, LANES), F32),
-        pltpu.VMEM((CHIPS, 2, NC, NZL, LANES), F32),
+        pltpu.VMEM((4, OWNERS, 2, LANES), F32),
+        pltpu.VMEM((CHIPS, 4, 2, LANES), F32),
+        pltpu.VMEM((CHIPS, 6, 2, LANES), F32),
+        pltpu.VMEM((CHIPS, NC, 2, LANES), F32),
+        pltpu.VMEM((2, NC, OWNERS, 2, LANES), F32),
+        pltpu.VMEM((CHIPS, 2, NC, 2, LANES), F32),
+        pltpu.VMEM((CHIPS, 2, NC, 2, LANES), F32),
+        pltpu.VMEM((2, NC, OWNERS, 2, LANES), F32),
         pltpu.VMEM((2, NC, NZL, LANES), F32),
         pltpu.VMEM((CHIPS, NC, NZL, LANES), F32),
         pltpu.VMEM((NC, NZL, LANES), F32),
@@ -723,13 +924,23 @@
         pltpu.VMEM((LANES,), jnp.int32),
         pltpu.VMEM((LANES,), F32),
         pltpu.VMEM((LANES,), F32),
-        pltpu.SemaphoreType.DMA((5,)),
+        pltpu.SemaphoreType.DMA((6,)),
         pltpu.SemaphoreType.DMA((5,)),
         pltpu.SemaphoreType.DMA((5,)),
         pltpu.SemaphoreType.DMA((3,)),
         pltpu.SemaphoreType.DMA((3,)),
+        pltpu.SemaphoreType.REGULAR((3,)),
+        pltpu.SemaphoreType.REGULAR((5,)),
+        pltpu.SemaphoreType.DMA((2, 2)),
+        pltpu.SemaphoreType.DMA((2, 2)),
+        pltpu.SemaphoreType.DMA((3,)),
+        pltpu.SemaphoreType.DMA((3,)),
         pltpu.SemaphoreType.DMA((SWEEPS, 4)),
         pltpu.SemaphoreType.DMA((SWEEPS, 4)),
+        pltpu.SemaphoreType.DMA,
+        pltpu.SemaphoreType.DMA,
+        pltpu.SemaphoreType.DMA,
+        pltpu.SemaphoreType.DMA,
         pltpu.SemaphoreType.DMA,
         pltpu.SemaphoreType.DMA,
         pltpu.SemaphoreType.DMA((SWEEPS,)),
@@ -747,7 +958,7 @@
             jax.ShapeDtypeStruct((NC, NZL, NXL, NYL), F32),
             jax.ShapeDtypeStruct((LANES,), F32),
         ),
-        in_specs=[anywhere] * 7,
+        in_specs=[pl.BlockSpec(memory_space=pltpu.HBM)] * 7,
         out_specs=(anywhere, anywhere),
         scratch_shapes=scratch,
         compiler_params=pltpu.CompilerParams(

time: 54.2 us -> 52.3 us (0.965)
  Pallas kernels: 51.2 us -> 49.4 us
    pallas_call x1, Pallas kernels: 51.2 us -> 49.4 us  [shards(): pl.pallas_call(kernel, out_shape=(jax.ShapeDtypeStruct((NC, NZL, NXL, NYL...]
where the time goes in v3:
time: 52.3 us; the launch traced here: 52.2 us
  Pallas kernels  49.4 us (94%)
  local copies, waits for them, and re-layouts  2.21 us (4%)
  between operations  0.65 us (1%)
    pallas_call x1, Pallas kernels, shards(): pl.pallas_call(kernel, out_shape=(jax.ShapeDtypeStruct((NC, NZL, NXL, NYL...  49.4 us
    unnamed x4, local copies, waits for them, and re-layouts  2.21 us

profile of v3, /device:TPU:1, one launch (start us, length us, event | category | flops | bytes accessed | tf_op | source)
XLA Modules:
  0.0 52.2 jit_solution(14933279242512941506)
XLA Ops:
  0.6 49.4 %shard_map.86 = (f32[3,12,8,256]{3,2,1,0:T(8,128)}, f32[128]{0:T(128)}) custom-call(f32[3,12,8,256]{3,2,1,0:T(8,128)} %bitcast.6, f32[3,12,8,256]{3,2,1,0:T(8,128)} %bitcast.7, f32[12,8,256]{2,1,0:T(8,128)} %bitcast.10, f32[3,12,8,256]{3,2,1,0:T(8,128)} %bitcast.8, s32[12,8,256]{2,1,0:T(8,128)} %bitcast.11, s32[128]{0:T(128)} %tb_h.1, f32[128]{0:T(128)} %tw_h.1), custom_call_target="tpu_custom_call" | custom-call | tf_op jit(solution)/shard_map/pallas_call | solution.py:955
  50.0 0.0 copy-start
  50.0 1.7 %copy.11 = f32[3,8,12,256]{3,1,2,0:T(8,128)} copy(f32[3,8,12,256]{3,1,2,0:T(8,128)} %bitcast.9) | data formatting | bytes 589824
  51.7 0.0 copy-done
  51.7 0.5 copy.12
Async XLA Ops:
  50.0 1.7 %copy-start = (f32[128]{0:T(128)S(1)}, f32[128]{0:T(128)}, u32[]{:S(2)}) copy-start(f32[128]{0:T(128)} %get-tuple-element.9) | copy-start | bytes 1540

commit v4 on v3

--- a/solution.py
+++ b/solution.py
@@ -68,7 +68,7 @@
     MS,
     MR,
     CB,
-    CG,
+    CE,
     OWN,
     QS,
     QR,
@@ -80,11 +80,12 @@
     R1,
     S2,
     R2,
+    E2,
+    RE,
     AL,
     AR,
-    SH,
-    SL,
-    OHB,
+    OHH,
+    OHL,
     B1S,
     B1R,
     B2S,
@@ -113,6 +114,8 @@
     d_recv,
     p_send,
     p_recv,
+    e_send,
+    e_recv,
     b_send,
     b_recv,
 ):
@@ -505,8 +508,9 @@
     first = lane == 0
     last = lane == LANES - 1
 
-    def eliminate(s, A):
-        edges = [[YR[s, side, h] for h in range(2)] for side in range(2)]
+    def eliminate(s, A, low, count, unroll):
+        if s is not None:
+            edges = [[YR[s, side, h] for h in range(2)] for side in range(2)]
 
         def plane(z, carry):
             cross = []
@@ -536,8 +540,10 @@
                 for h in range(2):
                     south, north, below, above = cross[h]
                     a = A[c, z + 1, h]
-                    lo = pltpu.roll(edges[0][h], lax.rem(LANES - k, LANES), 1)
-                    hi = pltpu.roll(edges[1][h], LANES - 1 - k, 1)
+                    lo = hi = blank
+                    if s is not None:
+                        lo = pltpu.roll(edges[0][h], lax.rem(LANES - k, LANES), 1)
+                        hi = pltpu.roll(edges[1][h], LANES - 1 - k, 1)
                     y_lo = jnp.where(first, lo, pltpu.roll(a, 1, 1))
                     y_hi = jnp.where(last, hi, pltpu.roll(a, LANES - 1, 1))
                     rhs = SRC[c, z, h] + shift_coef * a
@@ -554,14 +560,14 @@
                     PP[c, z, h] = p[h]
             return carry
 
-        lax.fori_loop(0, NZL, plane, 0)
+        lax.fori_loop(low, low + count, plane, 0, unroll=unroll)
 
     own_copies[0].wait()
     side_copies[0].wait_recv()
     first_arrivals()
     pl.semaphore_wait(LP.at[0], v_near)
     call_line(LP.at[1], True)
-    eliminate(0, A1)
+    eliminate(0, A1, 0, NZL, 12)
     for c in range(NC):
         for i, x in enumerate((0, NXC - 1)):
             value = level(p2, x, c)
@@ -574,16 +580,17 @@
 
     own_copies[4].wait()
     side_copies[4].wait_recv()
-    iota16 = lax.broadcasted_iota(jnp.int32, (16, LANES), 0)
+
+    def indicator(digit):
+        return jnp.concatenate(
+            [jnp.where(digit == i, 1.0, 0.0) for i in range(16)], axis=0
+        ).astype(jnp.bfloat16)
 
     def onehot(z, carry):
         for h in range(2):
-            low_part = lax.rem(BAND[z, h], 16)
-            for i in range(8):
-                at = (8 * h + i) * LANES
-                OHB[z, :, at : at + LANES] = jnp.where(
-                    jnp.broadcast_to(low_part[i : i + 1], (16, LANES)) == iota16, 1.0, 0.0
-                ).astype(jnp.bfloat16)
+            cut = slice(h * LANES, (h + 1) * LANES)
+            OHL[z, :, cut] = indicator(lax.rem(BAND[z, h], 16))
+            OHH[z, :, cut] = indicator(BAND[z, h] // 16)
         return carry
 
     lax.fori_loop(0, NZL, onehot, 0)
@@ -633,12 +640,32 @@
 
     arrive(MR, m_recv)
 
+    row_z = lax.broadcasted_iota(jnp.int32, (NZL, LANES), 0)
+    lane_z = lax.broadcasted_iota(jnp.int32, (NZL, LANES), 1)
+
+    def write_edges(ref, values):
+        packed = jnp.zeros((NZL, LANES), F32)
+        for c in range(NC):
+            v = values[c]
+            for side in range(2):
+                ref[2 * c + side : 2 * c + side + 1, :] = v[
+                    side * (NZL - 1) : side * (NZL - 1) + 1
+                ]
+                column = v[:, side * (LANES - 1) : side * (LANES - 1) + 1]
+                packed = jnp.where(
+                    lane_z == NZL * (2 * c + side) + row_z,
+                    jnp.broadcast_to(column, (NZL, LANES)),
+                    packed,
+                )
+        ref[6:7, :] = jnp.sum(packed, axis=0, keepdims=True)
+        ref[7:8, :] = jnp.zeros((1, LANES), F32)
+
     def upstream(k, F):
         lf, lg, rf, rg = (MR[k, i] for i in range(4))
         b = lg / (1.0 - lf * F)
         g = b * F
         CB[k] = b
-        CG[k] = g
+        write_edges(CE.at[k], (b, b, b))
         return rg + g * rf
 
     def downstream(i, H):
@@ -647,7 +674,7 @@
         b = rf / (1.0 - rg * H)
         g = b * H
         CB[k] = b
-        CG[k] = g
+        write_edges(CE.at[k], (b, b, b))
         return lf + g * lg
 
     none = jnp.zeros((NZL, LANES), F32)
@@ -704,37 +731,82 @@
             packs = pack_edges(c * NZL + z, pair, packs)
         return packs
 
-    halo2 = send_halo(1, A2, lax.fori_loop(0, NZL, line_first, no_packs))
+    halo2 = send_halo(1, A2, lax.fori_loop(0, NZL, line_first, no_packs, unroll=4))
+
+    def ends(write):
+        for c in range(NC):
+            first_p = level(p2, 0, c)
+            last_p = level(p2, NXC - 1, c)
+            write(c, last_p + OWN[6] * first_p, first_p + OWN[7] * last_p)
+
+    def write_rows(c, up, down):
+        S2[0, c] = up
+        S2[1, c] = down
+
+    def side_of(target):
+        return jnp.where(target > chip, 0, 1)
+
+    eliminate(None, A2, 1, NZL - 2, 5)
+    ends(write_rows)
+    to_chips(lambda target: S2.at[side_of(target)], R2, p_send.at[1], p_recv.at[1])
 
     each(halo2, 2, lambda c: c.wait_recv())
     pl.semaphore_wait(LP.at[3], p_near)
     call_line(LP.at[4], False)
-    eliminate(1, A2)
-    for c in range(NC):
-        first_p = level(p2, 0, c)
-        last_p = level(p2, NXC - 1, c)
-        S2[0, c] = last_p + OWN[6] * first_p
-        S2[1, c] = first_p + OWN[7] * last_p
-    to_chips(
-        lambda target: S2.at[jnp.where(target > chip, 0, 1)], R2, p_send.at[1], p_recv.at[1]
-    )
+    eliminate(1, A2, 0, NZL, 12)
+    final = ([], [])
+
+    def keep_ends(c, up, down):
+        final[0].append(up)
+        final[1].append(down)
+
+    ends(keep_ends)
+    for i in range(2):
+        write_edges(E2.at[i], final[i])
+    to_chips(lambda target: E2.at[side_of(target)], RE, e_send, e_recv)
     arrive(R2, p_recv.at[1])
-
-    def up_second(k, O):
-        return tuple(R2[k, c] + CB[k] * O[c] for c in range(NC))
-
-    def down_second(i, Q):
-        k = CHIPS - 1 - i
-        return tuple(R2[k, c] + CB[k] * Q[c] for c in range(NC))
+    arrive(RE, e_recv)
+
+    def bring(k, carry):
+        O, edge = carry
+        return (
+            tuple(R2[k, c] + CB[k] * O[c] for c in range(NC)),
+            RE[k] + CE[k] * edge,
+        )
+
+    def brought(steps, chip_of):
+        O, edge = lax.fori_loop(0, steps, lambda i, v: bring(chip_of(i), v), (trio, blank))
+        packed = jnp.broadcast_to(edge[6:7], (NZL, LANES))
+        whole = []
+        for c in range(NC):
+            value = O[c]
+            for side in range(2):
+                at = lane_z == NZL * (2 * c + side) + row_z
+                column = jnp.sum(jnp.where(at, packed, 0.0), axis=1, keepdims=True)
+                value = jnp.where(
+                    lane_z == side * (LANES - 1), jnp.broadcast_to(column, (NZL, LANES)), value
+                )
+            for side in range(2):
+                value = jnp.where(
+                    row_z == side * (NZL - 1),
+                    jnp.broadcast_to(edge[2 * c + side : 2 * c + side + 1], (NZL, LANES)),
+                    value,
+                )
+            whole.append(value)
+        return whole
 
     close(
         (
-            lax.fori_loop(0, chip, up_second, trio),
-            lax.fori_loop(0, CHIPS - 1 - chip, down_second, trio),
+            brought(chip, lambda i: i),
+            brought(CHIPS - 1 - chip, lambda i: CHIPS - 1 - i),
         )
     )
 
-    def line_last(z, carry):
+    pl.semaphore_wait(LT.at[2], 1)
+    pl.semaphore_wait(LP.at[4], p_near)
+
+    def line_last(z, acc):
+        parts = ([], [])
         for h in range(2):
             total = None
             for c in range(NC):
@@ -744,43 +816,33 @@
                 total = term if total is None else total + term
             total = total * PEN[z, h]
             coarse = total.astype(jnp.bfloat16).astype(F32)
-            SH[z, h] = coarse
-            SL[z, h] = total - coarse
-        return carry
-
-    lax.fori_loop(0, NZL, line_last, 0)
-    def band_rows(z, acc):
-        parts = []
-        for h in range(2):
-            high_part = BAND[z, h] // 16
-            coarse = SH[z, h]
-            fine = SL[z, h]
-            for i in range(8):
-                hit = jnp.broadcast_to(high_part[i : i + 1], (16, LANES)) == iota16
-                parts.append(
-                    jnp.concatenate(
-                        [
-                            jnp.where(hit, jnp.broadcast_to(v[i : i + 1], (16, LANES)), 0.0)
-                            for v in (coarse, fine)
-                        ],
-                        axis=0,
-                    ).astype(jnp.bfloat16)
-                )
-        weights = jnp.concatenate(parts, axis=1)
+            for part, value in zip(parts, (coarse, total - coarse)):
+                part.append(jnp.concatenate([value, value], axis=0).astype(jnp.bfloat16))
+        weights = jnp.concatenate(
+            [
+                jnp.concatenate([jnp.concatenate(part, axis=1)] * 8, axis=0) * OHH[z]
+                for part in parts
+            ],
+            axis=0,
+        )
         return acc + lax.dot_general(
-            weights, OHB[z], (((1,), (1,)), ((), ())), preferred_element_type=F32
+            weights, OHL[z], (((1,), (1,)), ((), ())), preferred_element_type=F32
         )
 
-    pl.semaphore_wait(LT.at[2], 1)
-    pl.semaphore_wait(LP.at[4], p_near)
-    acc = lax.fori_loop(0, NZL, band_rows, jnp.zeros((32, 16), F32))
-    sums = acc[0:16] + acc[16:32]
-    wide = jnp.concatenate([sums] * 8, axis=1)
-    keep = lane // 16 == row
-    for h in range(2):
-        B1S[h : h + 1, :] = jnp.sum(
-            jnp.where(keep, wide[8 * h : 8 * h + 8], 0.0), axis=0, keepdims=True
-        )
+    acc = lax.fori_loop(0, NZL, line_last, jnp.zeros((2 * LANES, LANES), F32), unroll=3)
+    acc = acc[0:LANES] + acc[LANES : 2 * LANES]
+    keep = lax.rem(lane, 8) == row
+    for r in range(2):
+        tall = blank
+        for j in range(8):
+            at = 8 * (8 * r + j)
+            line = jnp.sum(jnp.where(keep, acc[at : at + 8], 0.0), axis=0, keepdims=True)
+            tall = jnp.where(row == j, jnp.broadcast_to(line, (8, LANES)), tall)
+        for d in (1, 2, 4):
+            tall = tall + jnp.where(
+                lax.rem(lane // d, 2) == 0, pltpu.roll(tall, LANES - d, 1), pltpu.roll(tall, d, 1)
+            )
+        B1S[r : r + 1, :] = jnp.sum(jnp.where(keep, tall, 0.0), axis=0, keepdims=True)
 
     def band_round(r, own, slots, device_of, beside):
         def send(j, carry):
@@ -830,7 +892,8 @@
     tb_copy.wait()
     tw_copy.wait()
     tb = TB[...].reshape(1, LANES)
-    spot = jnp.broadcast_to(lax.rem(tb, LANES), (8, LANES))
+    spot = lax.rem(tb, 16) * 8 + lax.rem(tb // 16, 8)
+    spot = jnp.broadcast_to(spot, (8, LANES))
     low_half = jnp.take_along_axis(jnp.broadcast_to(bands[0:1], (8, LANES)), spot, axis=1)
     high_half = jnp.take_along_axis(jnp.broadcast_to(bands[1:2], (8, LANES)), spot, axis=1)
     picked = jnp.where(tb < LANES, low_half[0:1], high_half[0:1])
@@ -860,6 +923,7 @@
         drain(CHIPS - 1, D1.at[0], d_send)
 
     drain(CHIPS - 1, S2.at[0], p_send.at[1])
+    drain(CHIPS - 1, E2.at[0], e_send)
     for r, own in enumerate((B1S, B2S)):
         drain(STREAM - 1, own, b_send.at[r])
     out_own.wait()
@@ -900,7 +964,7 @@
         pltpu.VMEM((4, NZL, LANES), F32),
         pltpu.VMEM((CHIPS, 4, NZL, LANES), F32),
         pltpu.VMEM((CHIPS, NZL, LANES), F32),
-        pltpu.VMEM((CHIPS, NZL, LANES), F32),
+        pltpu.VMEM((CHIPS, 8, LANES), F32),
         pltpu.VMEM((8, NZL, LANES), F32),
         pltpu.VMEM((4, OWNERS, 2, LANES), F32),
         pltpu.VMEM((CHIPS, 4, 2, LANES), F32),
@@ -912,11 +976,12 @@
         pltpu.VMEM((2, NC, OWNERS, 2, LANES), F32),
         pltpu.VMEM((2, NC, NZL, LANES), F32),
         pltpu.VMEM((CHIPS, NC, NZL, LANES), F32),
+        pltpu.VMEM((2, 8, LANES), F32),
+        pltpu.VMEM((CHIPS, 8, LANES), F32),
         pltpu.VMEM((NC, NZL, LANES), F32),
         pltpu.VMEM((NC, NZL, LANES), F32),
-        field(),
-        field(),
-        pltpu.VMEM((NZL, 16, NXC * LANES), jnp.bfloat16),
+        pltpu.VMEM((NZL, LANES, 2 * LANES), jnp.bfloat16),
+        pltpu.VMEM((NZL, LANES, 2 * LANES), jnp.bfloat16),
         pltpu.VMEM((2, LANES), F32),
         pltpu.VMEM((STREAM, 2, LANES), F32),
         pltpu.VMEM((2, LANES), F32),
@@ -945,6 +1010,8 @@
         pltpu.SemaphoreType.DMA,
         pltpu.SemaphoreType.DMA((SWEEPS,)),
         pltpu.SemaphoreType.DMA((SWEEPS,)),
+        pltpu.SemaphoreType.DMA,
+        pltpu.SemaphoreType.DMA,
         pltpu.SemaphoreType.DMA((2,)),
         pltpu.SemaphoreType.DMA((2,)),
     ]

time: 52.3 us -> 47.8 us (0.914)
  Pallas kernels: 49.4 us -> 44.9 us
    pallas_call x1, Pallas kernels: 49.4 us -> 44.9 us  [shards(): pl.pallas_call(kernel, out_shape=(jax.ShapeDtypeStruct((NC, NZL, NXL, NYL...]
where the time goes in v4:
time: 47.8 us; the launch traced here: 47.7 us
  Pallas kernels  44.9 us (94%)
  local copies, waits for them, and re-layouts  2.21 us (5%)
  between operations  0.65 us (1%)
    pallas_call x1, Pallas kernels, shards(): pl.pallas_call(kernel, out_shape=(jax.ShapeDtypeStruct((NC, NZL, NXL, NYL...  44.9 us
    unnamed x4, local copies, waits for them, and re-layouts  2.21 us

profile of v4, /device:TPU:1, one launch (start us, length us, event | category | flops | bytes accessed | tf_op | source)
XLA Modules:
  0.0 47.7 jit_solution(15110858331848436177)
XLA Ops:
  0.6 44.9 %shard_map.86 = (f32[3,12,8,256]{3,2,1,0:T(8,128)}, f32[128]{0:T(128)}) custom-call(f32[3,12,8,256]{3,2,1,0:T(8,128)} %bitcast.6, f32[3,12,8,256]{3,2,1,0:T(8,128)} %bitcast.7, f32[12,8,256]{2,1,0:T(8,128)} %bitcast.10, f32[3,12,8,256]{3,2,1,0:T(8,128)} %bitcast.8, s32[12,8,256]{2,1,0:T(8,128)} %bitcast.11, s32[128]{0:T(128)} %tb_h.1, f32[128]{0:T(128)} %tw_h.1), custom_call_target="tpu_custom_call" | custom-call | tf_op jit(solution)/shard_map/pallas_call | solution.py:1022
  45.5 0.0 copy-start
  45.5 1.7 %copy.11 = f32[3,8,12,256]{3,1,2,0:T(8,128)} copy(f32[3,8,12,256]{3,1,2,0:T(8,128)} %bitcast.9) | data formatting | bytes 589824
  47.2 0.0 copy-done
  47.2 0.5 %copy.12 = f32[128]{0:T(128)} copy(f32[128]{0:T(128)S(1)} %copy-done) | data formatting | bytes 1024
Async XLA Ops:
  45.5 1.7 %copy-start = (f32[128]{0:T(128)S(1)}, f32[128]{0:T(128)}, u32[]{:S(2)}) copy-start(f32[128]{0:T(128)} %get-tuple-element.9) | copy-start | bytes 1540

commit v5 on v4

--- a/solution.py
+++ b/solution.py
@@ -1029,16 +1029,21 @@
         out_specs=(anywhere, anywhere),
         scratch_shapes=scratch,
         compiler_params=pltpu.CompilerParams(
-            collective_id=0, has_side_effects=True, vmem_limit_bytes=56 * 1024 * 1024
+            collective_id=0, has_side_effects=True, vmem_limit_bytes=32 * 1024 * 1024
         ),
     )(
-        planes(adjoint_source),
-        planes(velocity),
-        planes(penalty),
-        planes(adjoint_start),
-        planes(cell_band),
-        tri_band,
-        tri_weight,
+        *(
+            pltpu.with_memory_space_constraint(x, pltpu.HBM)
+            for x in (
+                planes(adjoint_source),
+                planes(velocity),
+                planes(penalty),
+                planes(adjoint_start),
+                planes(cell_band),
+                tri_band,
+                tri_weight,
+            )
+        )
     )
     return planes(adjoint), tri_grad
 

time: 47.8 us -> 46.7 us (0.977)
  local copies, waits for them, and re-layouts: 2.21 us -> 1.23 us
    unnamed x4 -> x2, local copies, waits for them, and re-layouts: 2.21 us -> 1.23 us
where the time goes in v5:
time: 46.7 us; the launch traced here: 46.6 us
  Pallas kernels  44.7 us (96%)
  local copies, waits for them, and re-layouts  1.23 us (3%)
  between operations  0.64 us (1%)
    pallas_call x1, Pallas kernels, shards(): pl.pallas_call(kernel, out_shape=(jax.ShapeDtypeStruct((NC, NZL, NXL, NYL...  44.7 us
    unnamed x2, local copies, waits for them, and re-layouts  1.23 us

profile of v5, /device:TPU:1, one launch (start us, length us, event | category | flops | bytes accessed | tf_op | source)
XLA Modules:
  0.0 46.6 jit_solution(3522597305751888111)
XLA Ops:
  0.6 44.7 %shard_map.86 = (f32[3,12,8,256]{3,2,1,0:T(8,128)S(1)}, f32[128]{0:T(128)S(1)}) custom-call(f32[3,12,8,256]{3,2,1,0:T(8,128)} %bitcast.7, f32[3,12,8,256]{3,2,1,0:T(8,128)} %bitcast.8, f32[12,8,256]{2,1,0:T(8,128)} %bitcast.10, f32[3,12,8,256]{3,2,1,0:T(8,128)} %bitcast.9, s32[12,8,256]{2,1,0:T(8,128)} %bitcast.11, s32[128]{0:T(128)} %tb_h.1, f32[128]{0:T(128)} %tw_h.1), custom_call_target="tpu_custom_call" | custom-call | tf_op jit(solution)/shard_map/pallas_call | solution.py:1022
  45.4 0.7 %copy.11 = f32[3,8,12,256]{3,1,2,0:T(8,128)} copy(f32[3,8,12,256]{3,1,2,0:T(8,128)S(1)} %bitcast.6) | data formatting | bytes 589824
  46.1 0.5 %copy.12 = f32[128]{0:T(128)} copy(f32[128]{0:T(128)S(1)} %get-tuple-element.9) | data formatting | bytes 1024

commit v6 on v5

--- a/solution.py
+++ b/solution.py
@@ -219,25 +219,37 @@
         own_copies[i].start()
     tb_copy.start()
     tw_copy.start()
+    row = lax.broadcasted_iota(jnp.int32, (8, LANES), 0)
+    lane = lax.broadcasted_iota(jnp.int32, (8, LANES), 1)
+
+    def pack_edges(k, pair, packs):
+        low, high = packs
+        hit = lane == k
+        low = tuple(jnp.where(hit, pltpu.roll(pair[h], k, 1), low[h]) for h in range(2))
+        high = tuple(jnp.where(hit, pltpu.roll(pair[h], k + 1, 1), high[h]) for h in range(2))
+        return low, high
+
+    blank = jnp.zeros((8, LANES), F32)
+    no_packs = ((blank, blank), (blank, blank))
+
+    stage.wait()
+
+    def pack_start(z, packs):
+        low, high = packs
+        for c in range(NC):
+            pair = (STG[c, z, :, 0:LANES], STG[c, z, :, LANES:NYL])
+            low, high = pack_edges(c * NZL + z, pair, (low, high))
+        return low, high
+
+    low, high = lax.fori_loop(0, NZL, pack_start, no_packs, unroll=4)
+    for i, value in enumerate((low[0], high[1], high[0], low[1])):
+        YF[i] = value
     pl.semaphore_wait(barrier, 3 + 2 * v_near + 2 * p_near)
     for i in range(3):
         side_copies[i].start()
     call(LT.at[0], stream_at(-1))
     call(LT.at[0], stream_at(1))
     call_line(LP.at[0], True)
-
-    row = lax.broadcasted_iota(jnp.int32, (8, LANES), 0)
-    lane = lax.broadcasted_iota(jnp.int32, (8, LANES), 1)
-
-    def pack_edges(k, pair, packs):
-        low, high = packs
-        hit = lane == k
-        low = tuple(jnp.where(hit, pltpu.roll(pair[h], k, 1), low[h]) for h in range(2))
-        high = tuple(jnp.where(hit, pltpu.roll(pair[h], k + 1, 1), high[h]) for h in range(2))
-        return low, high
-
-    blank = jnp.zeros((8, LANES), F32)
-    no_packs = ((blank, blank), (blank, blank))
 
     def send_halo(s, A, packs):
         for side in range(2):
@@ -297,18 +309,6 @@
     for copy, there in first_halo:
         pl.when(there)(copy.start)
 
-    stage.wait()
-
-    def pack_start(z, packs):
-        low, high = packs
-        for c in range(NC):
-            pair = (STG[c, z, :, 0:LANES], STG[c, z, :, LANES:NYL])
-            low, high = pack_edges(c * NZL + z, pair, (low, high))
-        return low, high
-
-    low, high = lax.fori_loop(0, NZL, pack_start, no_packs)
-    for i, value in enumerate((low[0], high[1], high[0], low[1])):
-        YF[i] = value
     for i, step in enumerate((-1, 1)):
         copy = pltpu.make_async_remote_copy(
             src_ref=YF.at[i],
@@ -350,6 +350,10 @@
     for i in (1, 2):
         own_copies[i].wait()
         side_copies[i].wait_recv()
+
+    pl.semaphore_wait(LT.at[0], 2)
+    call(LT.at[1], stream_at(-2))
+    call(LT.at[1], stream_at(2))
 
     def flat(ref):
         count = 1
@@ -462,9 +466,6 @@
         got = slots.at[pl.ds(1, CHIPS - 1)]
         pltpu.make_async_copy(got, got, sem).wait()
 
-    pl.semaphore_wait(LT.at[0], 2)
-    call(LT.at[1], stream_at(-2))
-    call(LT.at[1], stream_at(2))
     pl.semaphore_wait(LT.at[1], 2)
     call(LT.at[2], (partner, mv, mp))
 
@@ -581,16 +582,16 @@
     own_copies[4].wait()
     side_copies[4].wait_recv()
 
-    def indicator(digit):
+    def indicator(digit, count):
         return jnp.concatenate(
-            [jnp.where(digit == i, 1.0, 0.0) for i in range(16)], axis=0
+            [jnp.where(digit == i, 1.0, 0.0) for i in range(count)], axis=0
         ).astype(jnp.bfloat16)
 
     def onehot(z, carry):
         for h in range(2):
             cut = slice(h * LANES, (h + 1) * LANES)
-            OHL[z, :, cut] = indicator(lax.rem(BAND[z, h], 16))
-            OHH[z, :, cut] = indicator(BAND[z, h] // 16)
+            OHL[z, :, cut] = indicator(lax.rem(BAND[z, h], 32), 32)
+            OHH[z, :, cut] = indicator(BAND[z, h] // 32, 8)
         return carry
 
     lax.fori_loop(0, NZL, onehot, 0)
@@ -665,7 +666,6 @@
         b = lg / (1.0 - lf * F)
         g = b * F
         CB[k] = b
-        write_edges(CE.at[k], (b, b, b))
         return rg + g * rf
 
     def downstream(i, H):
@@ -674,7 +674,6 @@
         b = rf / (1.0 - rg * H)
         g = b * H
         CB[k] = b
-        write_edges(CE.at[k], (b, b, b))
         return lf + g * lg
 
     none = jnp.zeros((NZL, LANES), F32)
@@ -750,6 +749,13 @@
     ends(write_rows)
     to_chips(lambda target: S2.at[side_of(target)], R2, p_send.at[1], p_recv.at[1])
 
+    def edge_coefficients(k, carry):
+        write_edges(CE.at[k], (CB[k],) * NC)
+        return carry
+
+    lax.fori_loop(0, chip, edge_coefficients, 0)
+    lax.fori_loop(chip + 1, CHIPS, edge_coefficients, 0)
+
     each(halo2, 2, lambda c: c.wait_recv())
     pl.semaphore_wait(LP.at[3], p_near)
     call_line(LP.at[4], False)
@@ -820,7 +826,7 @@
                 part.append(jnp.concatenate([value, value], axis=0).astype(jnp.bfloat16))
         weights = jnp.concatenate(
             [
-                jnp.concatenate([jnp.concatenate(part, axis=1)] * 8, axis=0) * OHH[z]
+                jnp.concatenate([jnp.concatenate(part, axis=1)] * 4, axis=0) * OHH[z]
                 for part in parts
             ],
             axis=0,
@@ -829,14 +835,14 @@
             weights, OHL[z], (((1,), (1,)), ((), ())), preferred_element_type=F32
         )
 
-    acc = lax.fori_loop(0, NZL, line_last, jnp.zeros((2 * LANES, LANES), F32), unroll=3)
-    acc = acc[0:LANES] + acc[LANES : 2 * LANES]
+    acc = lax.fori_loop(0, NZL, line_last, jnp.zeros((LANES, 2 * LANES), F32), unroll=12)
+    acc = acc[0:64] + acc[64:128]
     keep = lax.rem(lane, 8) == row
     for r in range(2):
         tall = blank
         for j in range(8):
-            at = 8 * (8 * r + j)
-            line = jnp.sum(jnp.where(keep, acc[at : at + 8], 0.0), axis=0, keepdims=True)
+            tile = acc[8 * j : 8 * j + 8, r * LANES : (r + 1) * LANES]
+            line = jnp.sum(jnp.where(keep, tile, 0.0), axis=0, keepdims=True)
             tall = jnp.where(row == j, jnp.broadcast_to(line, (8, LANES)), tall)
         for d in (1, 2, 4):
             tall = tall + jnp.where(
@@ -892,11 +898,11 @@
     tb_copy.wait()
     tw_copy.wait()
     tb = TB[...].reshape(1, LANES)
-    spot = lax.rem(tb, 16) * 8 + lax.rem(tb // 16, 8)
+    spot = lax.rem(tb, 16) * 8 + tb // 32
     spot = jnp.broadcast_to(spot, (8, LANES))
     low_half = jnp.take_along_axis(jnp.broadcast_to(bands[0:1], (8, LANES)), spot, axis=1)
     high_half = jnp.take_along_axis(jnp.broadcast_to(bands[1:2], (8, LANES)), spot, axis=1)
-    picked = jnp.where(tb < LANES, low_half[0:1], high_half[0:1])
+    picked = jnp.where(lax.rem(tb, 32) < 16, low_half[0:1], high_half[0:1])
     TRI[...] = (TW[...].reshape(1, LANES) * picked).reshape(LANES)
     tri_copy = pltpu.make_async_copy(TRI, tri_h, tri_sem.at[2])
     tri_copy.start()
@@ -980,8 +986,8 @@
         pltpu.VMEM((CHIPS, 8, LANES), F32),
         pltpu.VMEM((NC, NZL, LANES), F32),
         pltpu.VMEM((NC, NZL, LANES), F32),
-        pltpu.VMEM((NZL, LANES, 2 * LANES), jnp.bfloat16),
-        pltpu.VMEM((NZL, LANES, 2 * LANES), jnp.bfloat16),
+        pltpu.VMEM((NZL, 64, 2 * LANES), jnp.bfloat16),
+        pltpu.VMEM((NZL, 2 * LANES, 2 * LANES), jnp.bfloat16),
         pltpu.VMEM((2, LANES), F32),
         pltpu.VMEM((STREAM, 2, LANES), F32),
         pltpu.VMEM((2, LANES), F32),

time: 46.7 us -> 45.6 us (0.976)
  Pallas kernels: 44.7 us -> 43.6 us
    pallas_call x1, Pallas kernels: 44.7 us -> 43.6 us  [shards(): pl.pallas_call(kernel, out_shape=(jax.ShapeDtypeStruct((NC, NZL, NXL, NYL...]
where the time goes in v6:
time: 45.6 us; the launch traced here: 45.5 us
  Pallas kernels  43.6 us (96%)
  local copies, waits for them, and re-layouts  1.23 us (3%)
  between operations  0.64 us (1%)
    pallas_call x1, Pallas kernels, shards(): pl.pallas_call(kernel, out_shape=(jax.ShapeDtypeStruct((NC, NZL, NXL, NYL...  43.6 us
    unnamed x2, local copies, waits for them, and re-layouts  1.23 us

profile of v6, /device:TPU:1, one launch (start us, length us, event | category | flops | bytes accessed | tf_op | source)
XLA Modules:
  0.0 45.5 jit_solution(13935763637655633233)
XLA Ops:
  0.6 43.6 %shard_map.86 = (f32[3,12,8,256]{3,2,1,0:T(8,128)S(1)}, f32[128]{0:T(128)S(1)}) custom-call(f32[3,12,8,256]{3,2,1,0:T(8,128)} %bitcast.7, f32[3,12,8,256]{3,2,1,0:T(8,128)} %bitcast.8, f32[12,8,256]{2,1,0:T(8,128)} %bitcast.10, f32[3,12,8,256]{3,2,1,0:T(8,128)} %bitcast.9, s32[12,8,256]{2,1,0:T(8,128)} %bitcast.11, s32[128]{0:T(128)} %tb_h.1, f32[128]{0:T(128)} %tw_h.1), custom_call_target="tpu_custom_call" | custom-call | tf_op jit(solution)/shard_map/pallas_call | solution.py:1028
  44.2 0.7 %copy.11 = f32[3,8,12,256]{3,1,2,0:T(8,128)} copy(f32[3,8,12,256]{3,1,2,0:T(8,128)S(1)} %bitcast.6) | data formatting | bytes 589824
  45.0 0.5 %copy.12 = f32[128]{0:T(128)} copy(f32[128]{0:T(128)S(1)} %get-tuple-element.9) | data formatting | bytes 1024

commit v7 on v6

--- a/solution.py
+++ b/solution.py
@@ -21,6 +21,7 @@
 NYL = 256
 LANES = 128
 OWNERS = 6
+FAR_FIRST = (4, 3, 5, 2, 6, 1, 7)
 
 stream_coef = 1000.0
 stream_conv = 200.0
@@ -41,7 +42,7 @@
     tb_h,
     tw_h,
     out_h,
-    tri_h,
+    tri_ref,
     SRC,
     VEL,
     PEN,
@@ -92,7 +93,6 @@
     B2R,
     TB,
     TW,
-    TRI,
     in_sem,
     side_send,
     side_recv,
@@ -448,7 +448,7 @@
         MS[2 * k + 1] = level(ref2, NXC - 1)
 
     def to_chips(src_of, dst, send_sem, recv_sem):
-        def send(j, carry):
+        for j in FAR_FIRST:
             target = lax.rem(chip + j, CHIPS)
             pltpu.make_async_remote_copy(
                 src_ref=src_of(target),
@@ -458,9 +458,6 @@
                 device_id=(2 * target + q, mv, mp),
                 device_id_type=MESH,
             ).start()
-            return carry
-
-        lax.fori_loop(1, CHIPS, send, 0)
 
     def arrive(slots, sem):
         got = slots.at[pl.ds(1, CHIPS - 1)]
@@ -474,10 +471,11 @@
     owner_sends = jnp.where(is_owner, OWNERS - 1, OWNERS)
 
     def to_owners(src_of, dst, send_sem, recv_sem):
-        def send(o, carry):
-            target = o + o // 3
-
-            @pl.when(target != chip)
+        for j in FAR_FIRST:
+            target = lax.rem(chip + j, CHIPS)
+            o = (target // 4) * 3 + lax.rem(target, 4)
+
+            @pl.when(lax.rem(target, 4) < 3)
             def _():
                 pltpu.make_async_remote_copy(
                     src_ref=src_of(o),
@@ -488,13 +486,9 @@
                     device_id_type=MESH,
                 ).start()
 
-            @pl.when(target == chip)
-            def _():
-                pltpu.make_async_copy(src_of(o), dst, recv_sem).start()
-
-            return carry
-
-        lax.fori_loop(0, OWNERS, send, 0)
+        @pl.when(is_owner)
+        def _():
+            pltpu.make_async_copy(src_of(my_o), dst, recv_sem).start()
 
     for k in range(4):
         value = MS[k]
@@ -624,7 +618,7 @@
                 after[c] = CO[k, 2] * G1[k, 0, c] + CO[k, 3] * before + CO[k, 4] * after[c]
                 D1[k, 0, c] = CO[k, 5] * after[c] + before
 
-        def reply(j, carry):
+        for j in FAR_FIRST:
             target = lax.rem(chip + j, CHIPS)
             pltpu.make_async_remote_copy(
                 src_ref=D1.at[target],
@@ -634,9 +628,7 @@
                 device_id=(2 * target + q, mv, mp),
                 device_id_type=MESH,
             ).start()
-            return carry
-
-        lax.fori_loop(1, CHIPS, reply, 0)
+
         pltpu.make_async_copy(D1.at[chip], R1.at[:, :, my_o], d_recv).start()
 
     arrive(MR, m_recv)
@@ -850,8 +842,8 @@
             )
         B1S[r : r + 1, :] = jnp.sum(jnp.where(keep, tall, 0.0), axis=0, keepdims=True)
 
-    def band_round(r, own, slots, device_of, beside):
-        def send(j, carry):
+    def band_round(r, own, slots, order, device_of, beside):
+        for j in order:
             pltpu.make_async_remote_copy(
                 src_ref=own,
                 dst_ref=slots.at[j],
@@ -860,9 +852,6 @@
                 device_id=device_of(j),
                 device_id_type=MESH,
             ).start()
-            return carry
-
-        lax.fori_loop(1, STREAM, send, 0)
         beside()
         got = slots.at[pl.ds(1, STREAM - 1)]
         pltpu.make_async_copy(got, got, b_recv.at[r]).wait()
@@ -870,6 +859,16 @@
         for j in range(1, STREAM):
             total = total + slots[j]
         return total
+
+    def drain(count, ref, sem):
+        def one(j, carry):
+            pltpu.make_async_copy(ref, ref, sem).wait()
+            return carry
+
+        lax.fori_loop(0, count, one, 0)
+
+    def sent(bytes_like, sem):
+        pltpu.make_async_copy(bytes_like, bytes_like, sem).wait()
 
     out_own = pltpu.make_async_copy(A3.at[:, :, q], out_h.at[:, :, :, lanes_of(q)], out_sem.at[0])
     out_side = pltpu.make_async_remote_copy(
@@ -881,60 +880,57 @@
         device_id_type=MESH,
     )
 
-    def send_out():
+    def beside_first():
         out_own.start()
         out_side.start()
-
-    B2S[...] = band_round(0, B1S, B1R, lambda j: (lax.rem(me + j, STREAM), mv, mp), send_out)
+        for copy in side_copies:
+            copy.wait_send()
+        for copy, there in first_halo:
+            pl.when(there)(copy.wait_send)
+        middle.wait_send()
+        each(halo2, 1, lambda c: c.wait_send())
+        others = pl.ds(1, CHIPS - 1)
+        sent(MR.at[others], m_send)
+        sent(R2.at[others], p_send.at[1])
+        sent(RE.at[others], e_send)
+        drain(owner_sends, QS.at[:, 0], q_send)
+        drain(owner_sends, S1.at[:, :, 0], p_send.at[0])
+
+        @pl.when(is_owner)
+        def _():
+            sent(D1.at[others], d_send)
+
+        tb_copy.wait()
+        tw_copy.wait()
+
+    def beside_second():
+        sent(B1R.at[pl.ds(1, STREAM - 1)], b_send.at[0])
+        out_own.wait()
+        out_side.wait()
+
+    line_order = (8, 7, 9, 6, 10, 5, 11, 4, 12, 3, 13, 2, 14, 1, 15)
+    plane_order = (10, 6, 9, 11, 14, 2, 8, 5, 7, 13, 15, 1, 3, 4, 12)
+    B2S[...] = band_round(
+        0, B1S, B1R, line_order, lambda j: (lax.rem(me + j, STREAM), mv, mp), beside_first
+    )
     bands = band_round(
         1,
         B2S,
         B2R,
+        plane_order,
         lambda j: (me, lax.rem(mv + j // SPAN, VERT), lax.rem(mp + j % SPAN, SPAN)),
-        lambda: None,
+        beside_second,
     )
     cells = STREAM * VERT * SPAN * NXL * NZL * NYL
     bands = bands * ((NBANDS / cells) ** 0.5)
-    tb_copy.wait()
-    tw_copy.wait()
     tb = TB[...].reshape(1, LANES)
     spot = lax.rem(tb, 16) * 8 + tb // 32
     spot = jnp.broadcast_to(spot, (8, LANES))
     low_half = jnp.take_along_axis(jnp.broadcast_to(bands[0:1], (8, LANES)), spot, axis=1)
     high_half = jnp.take_along_axis(jnp.broadcast_to(bands[1:2], (8, LANES)), spot, axis=1)
     picked = jnp.where(lax.rem(tb, 32) < 16, low_half[0:1], high_half[0:1])
-    TRI[...] = (TW[...].reshape(1, LANES) * picked).reshape(LANES)
-    tri_copy = pltpu.make_async_copy(TRI, tri_h, tri_sem.at[2])
-    tri_copy.start()
-
-    def drain(count, ref, sem):
-        def one(j, carry):
-            pltpu.make_async_copy(ref, ref, sem).wait()
-            return carry
-
-        lax.fori_loop(0, count, one, 0)
-
-    for copy in side_copies:
-        copy.wait_send()
-    for copy, there in first_halo:
-        pl.when(there)(copy.wait_send)
-    middle.wait_send()
-    each(halo2, 1, lambda c: c.wait_send())
-    drain(CHIPS - 1, MS, m_send)
-    drain(owner_sends, QS.at[:, 0], q_send)
-    drain(owner_sends, S1.at[:, :, 0], p_send.at[0])
-
-    @pl.when(is_owner)
-    def _():
-        drain(CHIPS - 1, D1.at[0], d_send)
-
-    drain(CHIPS - 1, S2.at[0], p_send.at[1])
-    drain(CHIPS - 1, E2.at[0], e_send)
-    for r, own in enumerate((B1S, B2S)):
-        drain(STREAM - 1, own, b_send.at[r])
-    out_own.wait()
-    out_side.wait()
-    tri_copy.wait()
+    tri_ref[...] = (TW[...].reshape(1, LANES) * picked).reshape(LANES)
+    sent(B2R.at[pl.ds(1, STREAM - 1)], b_send.at[1])
 
 
 def shards(adjoint_source, velocity, penalty, adjoint_start, cell_band, tri_band, tri_weight):
@@ -994,12 +990,11 @@
         pltpu.VMEM((STREAM, 2, LANES), F32),
         pltpu.VMEM((LANES,), jnp.int32),
         pltpu.VMEM((LANES,), F32),
-        pltpu.VMEM((LANES,), F32),
         pltpu.SemaphoreType.DMA((6,)),
         pltpu.SemaphoreType.DMA((5,)),
         pltpu.SemaphoreType.DMA((5,)),
         pltpu.SemaphoreType.DMA((3,)),
-        pltpu.SemaphoreType.DMA((3,)),
+        pltpu.SemaphoreType.DMA((2,)),
         pltpu.SemaphoreType.REGULAR((3,)),
         pltpu.SemaphoreType.REGULAR((5,)),
         pltpu.SemaphoreType.DMA((2, 2)),
@@ -1032,7 +1027,7 @@
             jax.ShapeDtypeStruct((LANES,), F32),
         ),
         in_specs=[pl.BlockSpec(memory_space=pltpu.HBM)] * 7,
-        out_specs=(anywhere, anywhere),
+        out_specs=(anywhere, pl.BlockSpec(memory_space=pltpu.VMEM)),
         scratch_shapes=scratch,
         compiler_params=pltpu.CompilerParams(
             collective_id=0, has_side_effects=True, vmem_limit_bytes=32 * 1024 * 1024

time: 45.6 us -> 44.9 us (0.985)
  Pallas kernels: 43.6 us -> 42.9 us
    pallas_call x1, Pallas kernels: 43.6 us -> 42.9 us  [shards(): pl.pallas_call(kernel, out_shape=(jax.ShapeDtypeStruct((NC, NZL, NXL, NYL...]
where the time goes in v7:
time: 44.9 us; the launch traced here: 44.8 us
  Pallas kernels  42.9 us (96%)
  local copies, waits for them, and re-layouts  1.23 us (3%)
  between operations  0.64 us (1%)
    pallas_call x1, Pallas kernels, shards(): pl.pallas_call(kernel, out_shape=(jax.ShapeDtypeStruct((NC, NZL, NXL, NYL...  42.9 us
    unnamed x2, local copies, waits for them, and re-layouts  1.23 us

profile of v7, /device:TPU:1, one launch (start us, length us, event | category | flops | bytes accessed | tf_op | source)
XLA Modules:
  0.0 44.8 jit_solution(13400032306548453548)
XLA Ops:
  0.6 42.9 %shard_map.86 = (f32[3,12,8,256]{3,2,1,0:T(8,128)S(1)}, f32[128]{0:T(128)S(1)}) custom-call(f32[3,12,8,256]{3,2,1,0:T(8,128)} %bitcast.7, f32[3,12,8,256]{3,2,1,0:T(8,128)} %bitcast.8, f32[12,8,256]{2,1,0:T(8,128)} %bitcast.10, f32[3,12,8,256]{3,2,1,0:T(8,128)} %bitcast.9, s32[12,8,256]{2,1,0:T(8,128)} %bitcast.11, s32[128]{0:T(128)} %tb_h.1, f32[128]{0:T(128)} %tw_h.1), custom_call_target="tpu_custom_call" | custom-call | tf_op jit(solution)/shard_map/pallas_call | solution.py:1023
  43.6 0.7 %copy.11 = f32[3,8,12,256]{3,1,2,0:T(8,128)} copy(f32[3,8,12,256]{3,1,2,0:T(8,128)S(1)} %bitcast.6) | data formatting | bytes 589824
  44.3 0.5 %copy.12 = f32[128]{0:T(128)} copy(f32[128]{0:T(128)S(1)} %get-tuple-element.9) | data formatting | bytes 1024

commit v8 on v7

--- a/solution.py
+++ b/solution.py
@@ -21,6 +21,8 @@
 NYL = 256
 LANES = 128
 OWNERS = 6
+ROWS = NZL // OWNERS
+FIRST = 2
 FAR_FIRST = (4, 3, 5, 2, 6, 1, 7)
 
 stream_coef = 1000.0
@@ -466,16 +468,16 @@
     pl.semaphore_wait(LT.at[1], 2)
     call(LT.at[2], (partner, mv, mp))
 
-    is_owner = lax.rem(chip, 4) < 3
-    my_o = (chip // 4) * 3 + lax.rem(chip, 4)
+    my_o = lax.rem(chip + FIRST, CHIPS)
+    is_owner = my_o < OWNERS
     owner_sends = jnp.where(is_owner, OWNERS - 1, OWNERS)
 
     def to_owners(src_of, dst, send_sem, recv_sem):
         for j in FAR_FIRST:
             target = lax.rem(chip + j, CHIPS)
-            o = (target // 4) * 3 + lax.rem(target, 4)
-
-            @pl.when(lax.rem(target, 4) < 3)
+            o = lax.rem(target + FIRST, CHIPS)
+
+            @pl.when(o < OWNERS)
             def _():
                 pltpu.make_async_remote_copy(
                     src_ref=src_of(o),
@@ -493,7 +495,7 @@
     for k in range(4):
         value = MS[k]
         for o in range(OWNERS):
-            QS[k, o] = value[2 * o : 2 * o + 2]
+            QS[k, o] = value[ROWS * o : ROWS * o + ROWS]
     to_owners(lambda o: QS.at[:, o], QR.at[chip], q_send, q_recv)
 
     for i in (3,):
@@ -567,7 +569,7 @@
         for i, x in enumerate((0, NXC - 1)):
             value = level(p2, x, c)
             for o in range(OWNERS):
-                S1[i, c, o] = value[2 * o : 2 * o + 2]
+                S1[i, c, o] = value[ROWS * o : ROWS * o + ROWS]
     to_owners(lambda o: S1.at[:, :, o], G1.at[chip], p_send.at[0], p_recv.at[0])
     pl.semaphore_wait(LP.at[1], v_near)
     call_line(LP.at[2], False)
@@ -593,7 +595,7 @@
     @pl.when(is_owner)
     def _():
         pltpu.make_async_copy(QR, QR, q_recv).wait()
-        ahead_f = jnp.zeros((2, LANES), F32)
+        ahead_f = jnp.zeros((ROWS, LANES), F32)
         for k in range(CHIPS):
             lf, lg, rf, rg = (QR[k, i] for i in range(4))
             inv = 1.0 / (1.0 - lf * ahead_f)
@@ -604,7 +606,7 @@
             ahead_f = rg + g * rf
 
         pltpu.make_async_copy(G1, G1, p_recv.at[0]).wait()
-        nil = jnp.zeros((2, LANES), F32)
+        nil = jnp.zeros((ROWS, LANES), F32)
         O = [nil] * NC
         for k in range(CHIPS):
             for c in range(NC):
@@ -711,8 +713,8 @@
     trio = (none,) * NC
     for c in range(NC):
         for o in range(OWNERS):
-            AL[c, 2 * o : 2 * o + 2, :] = R1[0, c, o]
-            AR[c, 2 * o : 2 * o + 2, :] = R1[1, c, o]
+            AL[c, ROWS * o : ROWS * o + ROWS, :] = R1[0, c, o]
+            AR[c, ROWS * o : ROWS * o + ROWS, :] = R1[1, c, o]
 
     def line_first(z, packs):
         for c in range(NC):
@@ -968,14 +970,14 @@
         pltpu.VMEM((CHIPS, NZL, LANES), F32),
         pltpu.VMEM((CHIPS, 8, LANES), F32),
         pltpu.VMEM((8, NZL, LANES), F32),
-        pltpu.VMEM((4, OWNERS, 2, LANES), F32),
-        pltpu.VMEM((CHIPS, 4, 2, LANES), F32),
-        pltpu.VMEM((CHIPS, 6, 2, LANES), F32),
-        pltpu.VMEM((CHIPS, NC, 2, LANES), F32),
-        pltpu.VMEM((2, NC, OWNERS, 2, LANES), F32),
-        pltpu.VMEM((CHIPS, 2, NC, 2, LANES), F32),
-        pltpu.VMEM((CHIPS, 2, NC, 2, LANES), F32),
-        pltpu.VMEM((2, NC, OWNERS, 2, LANES), F32),
+        pltpu.VMEM((4, OWNERS, ROWS, LANES), F32),
+        pltpu.VMEM((CHIPS, 4, ROWS, LANES), F32),
+        pltpu.VMEM((CHIPS, 6, ROWS, LANES), F32),
+        pltpu.VMEM((CHIPS, NC, ROWS, LANES), F32),
+        pltpu.VMEM((2, NC, OWNERS, ROWS, LANES), F32),
+        pltpu.VMEM((CHIPS, 2, NC, ROWS, LANES), F32),
+        pltpu.VMEM((CHIPS, 2, NC, ROWS, LANES), F32),
+        pltpu.VMEM((2, NC, OWNERS, ROWS, LANES), F32),
         pltpu.VMEM((2, NC, NZL, LANES), F32),
         pltpu.VMEM((CHIPS, NC, NZL, LANES), F32),
         pltpu.VMEM((2, 8, LANES), F32),

time: 44.9 us -> 43.7 us (0.973)
  Pallas kernels: 42.9 us -> 41.7 us
    pallas_call x1, Pallas kernels: 42.9 us -> 41.7 us  [shards(): pl.pallas_call(kernel, out_shape=(jax.ShapeDtypeStruct((NC, NZL, NXL, NYL...]
where the time goes in v8:
time: 43.7 us; the launch traced here: 43.6 us
  Pallas kernels  41.7 us (95%)
  local copies, waits for them, and re-layouts  1.23 us (3%)
  between operations  0.64 us (1%)
    pallas_call x1, Pallas kernels, shards(): pl.pallas_call(kernel, out_shape=(jax.ShapeDtypeStruct((NC, NZL, NXL, NYL...  41.7 us
    unnamed x2, local copies, waits for them, and re-layouts  1.23 us

profile of v8, /device:TPU:1, one launch (start us, length us, event | category | flops | bytes accessed | tf_op | source)
XLA Modules:
  0.0 43.6 jit_solution(7581547974336588640)
XLA Ops:
  0.6 41.7 %shard_map.86 = (f32[3,12,8,256]{3,2,1,0:T(8,128)S(1)}, f32[128]{0:T(128)S(1)}) custom-call(f32[3,12,8,256]{3,2,1,0:T(8,128)} %bitcast.7, f32[3,12,8,256]{3,2,1,0:T(8,128)} %bitcast.8, f32[12,8,256]{2,1,0:T(8,128)} %bitcast.10, f32[3,12,8,256]{3,2,1,0:T(8,128)} %bitcast.9, s32[12,8,256]{2,1,0:T(8,128)} %bitcast.11, s32[128]{0:T(128)} %tb_h.1, f32[128]{0:T(128)} %tw_h.1), custom_call_target="tpu_custom_call" | custom-call | tf_op jit(solution)/shard_map/pallas_call | solution.py:1025
  42.4 0.7 %copy.11 = f32[3,8,12,256]{3,1,2,0:T(8,128)} copy(f32[3,8,12,256]{3,1,2,0:T(8,128)S(1)} %bitcast.6) | data formatting | bytes 589824
  43.1 0.5 %copy.12 = f32[128]{0:T(128)} copy(f32[128]{0:T(128)S(1)} %get-tuple-element.9) | data formatting | bytes 1024

commit v9 on v8

--- a/solution.py
+++ b/solution.py
@@ -101,6 +101,7 @@
     out_sem,
     tri_sem,
     LT,
+    LD,
     LP,
     fz_send,
     fz_recv,
@@ -206,6 +207,23 @@
             A[c, NZL + 1] = nothing
     YR[...] = jnp.zeros(YR.shape, F32)
 
+    upper = chip >= CHIPS // 2
+    inside = (lax.rem(chip, 4) > 0, lax.rem(chip, 4) < 3)
+    in_near = either(inside[0]) + either(inside[1])
+    from_lower = either(upper) * (4 - either(jnp.logical_or(chip == 4, chip == 7)))
+
+    def chip_at(target):
+        return (2 * target + q, mv, mp)
+
+    def call_inside(sem):
+        for i, step in enumerate((-1, 1)):
+            pl.when(inside[i])(lambda: call(sem, chip_at(chip + step)))
+
+    for target in range(4, CHIPS):
+        apart = jnp.logical_and(chip != target - 1, lax.rem(target + 1, CHIPS) != chip)
+        pl.when(jnp.logical_and(jnp.logical_not(upper), apart))(
+            lambda: call(barrier, chip_at(target))
+        )
     call(barrier, (partner, mv, mp))
     call(barrier, stream_at(-1))
     call(barrier, stream_at(1))
@@ -246,11 +264,12 @@
     low, high = lax.fori_loop(0, NZL, pack_start, no_packs, unroll=4)
     for i, value in enumerate((low[0], high[1], high[0], low[1])):
         YF[i] = value
-    pl.semaphore_wait(barrier, 3 + 2 * v_near + 2 * p_near)
+    pl.semaphore_wait(barrier, 3 + 2 * v_near + 2 * p_near + from_lower)
     for i in range(3):
         side_copies[i].start()
-    call(LT.at[0], stream_at(-1))
-    call(LT.at[0], stream_at(1))
+    for target in range(4):
+        pl.when(upper)(lambda: call(LD, chip_at(target)))
+    call_inside(LT.at[0])
     call_line(LP.at[0], True)
 
     def send_halo(s, A, packs):
@@ -353,9 +372,8 @@
         own_copies[i].wait()
         side_copies[i].wait_recv()
 
-    pl.semaphore_wait(LT.at[0], 2)
-    call(LT.at[1], stream_at(-2))
-    call(LT.at[1], stream_at(2))
+    pl.semaphore_wait(LT.at[0], in_near)
+    call_inside(LT.at[1])
 
     def flat(ref):
         count = 1
@@ -465,7 +483,12 @@
         got = slots.at[pl.ds(1, CHIPS - 1)]
         pltpu.make_async_copy(got, got, sem).wait()
 
-    pl.semaphore_wait(LT.at[1], 2)
+    pl.semaphore_wait(LT.at[1], in_near)
+
+    @pl.when(jnp.logical_not(upper))
+    def _():
+        pl.semaphore_wait(LD, 4)
+
     call(LT.at[2], (partner, mv, mp))
 
     my_o = lax.rem(chip + FIRST, CHIPS)
@@ -998,6 +1021,7 @@
         pltpu.SemaphoreType.DMA((3,)),
         pltpu.SemaphoreType.DMA((2,)),
         pltpu.SemaphoreType.REGULAR((3,)),
+        pltpu.SemaphoreType.REGULAR,
         pltpu.SemaphoreType.REGULAR((5,)),
         pltpu.SemaphoreType.DMA((2, 2)),
         pltpu.SemaphoreType.DMA((2, 2)),

time: 43.7 us -> 43 us (0.984)
  Pallas kernels: 41.7 us -> 41.1 us
    pallas_call x1, Pallas kernels: 41.7 us -> 41.1 us  [shards(): pl.pallas_call(kernel, out_shape=(jax.ShapeDtypeStruct((NC, NZL, NXL, NYL...]
where the time goes in v9:
time: 43 us; the launch traced here: 42.9 us
  Pallas kernels  41.1 us (96%)
  local copies, waits for them, and re-layouts  1.23 us (3%)
  between operations  0.64 us (1%)
    pallas_call x1, Pallas kernels, shards(): pl.pallas_call(kernel, out_shape=(jax.ShapeDtypeStruct((NC, NZL, NXL, NYL...  41.1 us
    unnamed x2, local copies, waits for them, and re-layouts  1.23 us

profile of v9, /device:TPU:1, one launch (start us, length us, event | category | flops | bytes accessed | tf_op | source)
XLA Modules:
  0.0 42.9 jit_solution(11451638207558111056)
XLA Ops:
  0.6 41.1 %shard_map.86 = (f32[3,12,8,256]{3,2,1,0:T(8,128)S(1)}, f32[128]{0:T(128)S(1)}) custom-call(f32[3,12,8,256]{3,2,1,0:T(8,128)} %bitcast.7, f32[3,12,8,256]{3,2,1,0:T(8,128)} %bitcast.8, f32[12,8,256]{2,1,0:T(8,128)} %bitcast.10, f32[3,12,8,256]{3,2,1,0:T(8,128)} %bitcast.9, s32[12,8,256]{2,1,0:T(8,128)} %bitcast.11, s32[128]{0:T(128)} %tb_h.1, f32[128]{0:T(128)} %tw_h.1), custom_call_target="tpu_custom_call" | custom-call | tf_op jit(solution)/shard_map/pallas_call | solution.py:1049
  41.7 0.7 %copy.11 = f32[3,8,12,256]{3,1,2,0:T(8,128)} copy(f32[3,8,12,256]{3,1,2,0:T(8,128)S(1)} %bitcast.6) | data formatting | bytes 589824
  42.4 0.5 %copy.12 = f32[128]{0:T(128)} copy(f32[128]{0:T(128)S(1)} %get-tuple-element.9) | data formatting | bytes 1024

commit v10 on v9

--- a/solution.py
+++ b/solution.py
@@ -170,6 +170,10 @@
                 device_id_type=MESH,
             )
         )
+    stage = pltpu.make_async_copy(start_h, STG, in_sem.at[5])
+    stage.start()
+    for i in (1, 2, 0, 3, 4):
+        own_copies[i].start()
     tb_copy = pltpu.make_async_copy(tb_h, TB, tri_sem.at[0])
     tw_copy = pltpu.make_async_copy(tw_h, TW, tri_sem.at[1])
 
@@ -233,10 +237,6 @@
             pl.when(has_v[i])(lambda: call(barrier, (other, mv + step, mp)))
             pl.when(has_p[i])(lambda: call(barrier, (other, mv, mp + step)))
 
-    stage = pltpu.make_async_copy(start_h, STG, in_sem.at[5])
-    stage.start()
-    for i in (1, 2, 0, 3, 4):
-        own_copies[i].start()
     tb_copy.start()
     tw_copy.start()
     row = lax.broadcasted_iota(jnp.int32, (8, LANES), 0)
@@ -606,10 +606,19 @@
             [jnp.where(digit == i, 1.0, 0.0) for i in range(count)], axis=0
         ).astype(jnp.bfloat16)
 
+    digit32 = lax.broadcasted_iota(jnp.int32, (32, LANES), 0)
+
     def onehot(z, carry):
         for h in range(2):
             cut = slice(h * LANES, (h + 1) * LANES)
-            OHL[z, :, cut] = indicator(lax.rem(BAND[z, h], 32), 32)
+            low = lax.rem(BAND[z, h], 32)
+            OHL[z, :, cut] = jnp.concatenate(
+                [
+                    jnp.where(jnp.broadcast_to(low[x : x + 1], (32, LANES)) == digit32, 1.0, 0.0)
+                    for x in range(8)
+                ],
+                axis=0,
+            ).astype(jnp.bfloat16)
             OHH[z, :, cut] = indicator(BAND[z, h] // 32, 8)
         return carry
 
@@ -787,18 +796,22 @@
     for i in range(2):
         write_edges(E2.at[i], final[i])
     to_chips(lambda target: E2.at[side_of(target)], RE, e_send, e_recv)
+    ways = ((chip, lambda i: i), (CHIPS - 1 - chip, lambda i: CHIPS - 1 - i))
     arrive(R2, p_recv.at[1])
+
+    def bring(k, O):
+        return tuple(R2[k, c] + CB[k] * O[c] for c in range(NC))
+
+    rows_brought = [
+        lax.fori_loop(0, steps, lambda i, v: bring(chip_of(i), v), trio) for steps, chip_of in ways
+    ]
     arrive(RE, e_recv)
 
-    def bring(k, carry):
-        O, edge = carry
-        return (
-            tuple(R2[k, c] + CB[k] * O[c] for c in range(NC)),
-            RE[k] + CE[k] * edge,
-        )
-
-    def brought(steps, chip_of):
-        O, edge = lax.fori_loop(0, steps, lambda i, v: bring(chip_of(i), v), (trio, blank))
+    def brought(O, way):
+        steps, chip_of = way
+        edge = lax.fori_loop(
+            0, steps, lambda i, v: RE[chip_of(i)] + CE[chip_of(i)] * v, blank
+        )
         packed = jnp.broadcast_to(edge[6:7], (NZL, LANES))
         whole = []
         for c in range(NC):
@@ -820,8 +833,8 @@
 
     close(
         (
-            brought(chip, lambda i: i),
-            brought(CHIPS - 1 - chip, lambda i: CHIPS - 1 - i),
+            brought(rows_brought[0], ways[0]),
+            brought(rows_brought[1], ways[1]),
         )
     )
 
@@ -854,18 +867,19 @@
 
     acc = lax.fori_loop(0, NZL, line_last, jnp.zeros((LANES, 2 * LANES), F32), unroll=12)
     acc = acc[0:64] + acc[64:128]
-    keep = lax.rem(lane, 8) == row
+    keep = [lane // 32 + 4 * r == row for r in range(2)]
+    tall = blank
+    for j in range(8):
+        tile = acc[8 * j : 8 * j + 8]
+        own_x = jnp.where(keep[0], tile[:, 0:LANES], 0.0) + jnp.where(
+            keep[1], tile[:, LANES : 2 * LANES], 0.0
+        )
+        line = jnp.sum(own_x, axis=0, keepdims=True)
+        tall = jnp.where(row == j, jnp.broadcast_to(line, (8, LANES)), tall)
+    tall = tall + pltpu.roll(tall, 64, 1)
+    tall = tall + pltpu.roll(tall, 32, 1)
     for r in range(2):
-        tall = blank
-        for j in range(8):
-            tile = acc[8 * j : 8 * j + 8, r * LANES : (r + 1) * LANES]
-            line = jnp.sum(jnp.where(keep, tile, 0.0), axis=0, keepdims=True)
-            tall = jnp.where(row == j, jnp.broadcast_to(line, (8, LANES)), tall)
-        for d in (1, 2, 4):
-            tall = tall + jnp.where(
-                lax.rem(lane // d, 2) == 0, pltpu.roll(tall, LANES - d, 1), pltpu.roll(tall, d, 1)
-            )
-        B1S[r : r + 1, :] = jnp.sum(jnp.where(keep, tall, 0.0), axis=0, keepdims=True)
+        B1S[r : r + 1, :] = jnp.sum(jnp.where(keep[r], tall, 0.0), axis=0, keepdims=True)
 
     def band_round(r, own, slots, order, device_of, beside):
         for j in order:
@@ -880,10 +894,10 @@
         beside()
         got = slots.at[pl.ds(1, STREAM - 1)]
         pltpu.make_async_copy(got, got, b_recv.at[r]).wait()
-        total = own[...]
-        for j in range(1, STREAM):
-            total = total + slots[j]
-        return total
+        terms = [own[...]] + [slots[j] for j in range(1, STREAM)]
+        while len(terms) > 1:
+            terms = [terms[i] + terms[i + 1] for i in range(0, len(terms), 2)]
+        return terms[0]
 
     def drain(count, ref, sem):
         def one(j, carry):
@@ -949,11 +963,11 @@
     cells = STREAM * VERT * SPAN * NXL * NZL * NYL
     bands = bands * ((NBANDS / cells) ** 0.5)
     tb = TB[...].reshape(1, LANES)
-    spot = lax.rem(tb, 16) * 8 + tb // 32
+    spot = lax.rem(tb, LANES)
     spot = jnp.broadcast_to(spot, (8, LANES))
     low_half = jnp.take_along_axis(jnp.broadcast_to(bands[0:1], (8, LANES)), spot, axis=1)
     high_half = jnp.take_along_axis(jnp.broadcast_to(bands[1:2], (8, LANES)), spot, axis=1)
-    picked = jnp.where(lax.rem(tb, 32) < 16, low_half[0:1], high_half[0:1])
+    picked = jnp.where(tb < LANES, low_half[0:1], high_half[0:1])
     tri_ref[...] = (TW[...].reshape(1, LANES) * picked).reshape(LANES)
     sent(B2R.at[pl.ds(1, STREAM - 1)], b_send.at[1])
 

time: 43 us -> 42.5 us (0.988)
  Pallas kernels: 41.1 us -> 40.6 us
    pallas_call x1, Pallas kernels: 41.1 us -> 40.6 us  [shards(): pl.pallas_call(kernel, out_shape=(jax.ShapeDtypeStruct((NC, NZL, NXL, NYL...]
where the time goes in v10:
time: 42.5 us; the launch traced here: 42.4 us
  Pallas kernels  40.6 us (96%)
  local copies, waits for them, and re-layouts  1.23 us (3%)
  between operations  0.64 us (2%)
    pallas_call x1, Pallas kernels, shards(): pl.pallas_call(kernel, out_shape=(jax.ShapeDtypeStruct((NC, NZL, NXL, NYL...  40.6 us
    unnamed x2, local copies, waits for them, and re-layouts  1.23 us

profile of v10, /device:TPU:1, one launch (start us, length us, event | category | flops | bytes accessed | tf_op | source)
XLA Modules:
  0.0 42.4 jit_solution(11293310469702318909)
XLA Ops:
  0.6 40.6 %shard_map.86 = (f32[3,12,8,256]{3,2,1,0:T(8,128)S(1)}, f32[128]{0:T(128)S(1)}) custom-call(f32[3,12,8,256]{3,2,1,0:T(8,128)} %bitcast.7, f32[3,12,8,256]{3,2,1,0:T(8,128)} %bitcast.8, f32[12,8,256]{2,1,0:T(8,128)} %bitcast.10, f32[3,12,8,256]{3,2,1,0:T(8,128)} %bitcast.9, s32[12,8,256]{2,1,0:T(8,128)} %bitcast.11, s32[128]{0:T(128)} %tb_h.1, f32[128]{0:T(128)} %tw_h.1), custom_call_target="tpu_custom_call" | custom-call | tf_op jit(solution)/shard_map/pallas_call | solution.py:1063
  41.2 0.7 %copy.11 = f32[3,8,12,256]{3,1,2,0:T(8,128)} copy(f32[3,8,12,256]{3,1,2,0:T(8,128)S(1)} %bitcast.6) | data formatting | bytes 589824
  41.9 0.5 %copy.12 = f32[128]{0:T(128)} copy(f32[128]{0:T(128)S(1)} %get-tuple-element.9) | data formatting | bytes 1024

commit v11 on v10

--- a/solution.py
+++ b/solution.py
@@ -756,7 +756,7 @@
             packs = pack_edges(c * NZL + z, pair, packs)
         return packs
 
-    halo2 = send_halo(1, A2, lax.fori_loop(0, NZL, line_first, no_packs, unroll=4))
+    halo2 = send_halo(1, A2, lax.fori_loop(0, NZL, line_first, no_packs, unroll=12))
 
     def ends(write):
         for c in range(NC):
@@ -771,7 +771,7 @@
     def side_of(target):
         return jnp.where(target > chip, 0, 1)
 
-    eliminate(None, A2, 1, NZL - 2, 5)
+    eliminate(None, A2, 1, NZL - 2, 10)
     ends(write_rows)
     to_chips(lambda target: S2.at[side_of(target)], R2, p_send.at[1], p_recv.at[1])
 

time: 42.5 us -> 42.4 us (level)
  no operation moved by 1% of the time
where the time goes in v11:
time: 42.4 us; the launch traced here: 42.3 us
  Pallas kernels  40.4 us (95%)
  local copies, waits for them, and re-layouts  1.23 us (3%)
  between operations  0.64 us (2%)
    pallas_call x1, Pallas kernels, shards(): pl.pallas_call(kernel, out_shape=(jax.ShapeDtypeStruct((NC, NZL, NXL, NYL...  40.4 us
    unnamed x2, local copies, waits for them, and re-layouts  1.23 us

profile of v11, /device:TPU:1, one launch (start us, length us, event | category | flops | bytes accessed | tf_op | source)
XLA Modules:
  0.0 42.3 jit_solution(10866823634112129275)
XLA Ops:
  0.6 40.4 %shard_map.86 = (f32[3,12,8,256]{3,2,1,0:T(8,128)S(1)}, f32[128]{0:T(128)S(1)}) custom-call(f32[3,12,8,256]{3,2,1,0:T(8,128)} %bitcast.7, f32[3,12,8,256]{3,2,1,0:T(8,128)} %bitcast.8, f32[12,8,256]{2,1,0:T(8,128)} %bitcast.10, f32[3,12,8,256]{3,2,1,0:T(8,128)} %bitcast.9, s32[12,8,256]{2,1,0:T(8,128)} %bitcast.11, s32[128]{0:T(128)} %tb_h.1, f32[128]{0:T(128)} %tw_h.1), custom_call_target="tpu_custom_call" | custom-call | tf_op jit(solution)/shard_map/pallas_call | solution.py:1063
  41.0 0.7 %copy.11 = f32[3,8,12,256]{3,1,2,0:T(8,128)} copy(f32[3,8,12,256]{3,1,2,0:T(8,128)S(1)} %bitcast.6) | data formatting | bytes 589824
  41.8 0.5 %copy.12 = f32[128]{0:T(128)} copy(f32[128]{0:T(128)S(1)} %get-tuple-element.9) | data formatting | bytes 1024
